TPU v7x, 128 devices: a whole 4x4x4 slice. The times are simulated.
128 devices in a mesh: tok: 32 (over x, z, core), head: 4 (over y).
Axes of the slice: x: 4, y: 4, z: 4, core: 2. Of those that a mesh axis runs over, the one named last changes fastest.
Arguments:
- activations: bfloat16 [8192, 2048], P('tok'), may hold values from -6 to 6
- labels: int32 [8192], P('tok'), may hold values from 0 to 2
- position: int32 [8192], P('tok'), may hold values from 0 to 8191, as said below
- norm_gains: float32 [6, 2048], replicated, may hold values from 0.1 to 1.9
- qkv_weight: bfloat16 [2048, 3, 2048], P(None, None, 'head'), may hold values from -0.125 to 0.125
- out_weight: bfloat16 [2048, 2048], P('head'), may hold values from -0.75 to 0.75
- up_weight: bfloat16 [2048, 8192], P(None, 'head'), may hold values from -0.125 to 0.125
- down_weight: bfloat16 [8192, 2048], P('head'), may hold values from -0.09375 to 0.09375
- cotangent: bfloat16 [8192, 2048], P('tok'), may hold values from -6 to 6
Outputs:
- layer_out: bfloat16 [8192, 2048], P('tok')
- grad_input: float32 [8192, 2048], P('tok')
- grad_gains: float32 [6, 2048], P(None, 'tok')
- grad_qkv: float32 [2048, 3, 2048], P('tok', None, 'head')
- grad_out: float32 [2048, 2048], P(('head', 'tok'))
- grad_up: float32 [2048, 8192], P('tok', 'head')
- grad_down: float32 [8192, 2048], P(('head', 'tok'))
Inputs may be any that keep to these rules, and one draw needn't show every extreme that they name: position is a permutation of the 8192 places. Of the 256 rows of one device at most 16 have places in any one block of 256 consecutive places, and every device has exactly 16 in some block.
All inputs are finite; a program needn't handle non-finite values.
Results may differ from a plain program's by a relative error of at most 0.03.
Values may be sent and summed in bfloat16 or wider, within the bound.
A program may use at most 320 MiB of HBM per device.

v0:
```python
import functools
import math

import jax
import jax.numpy as jnp
from jax import lax
from jax.experimental import pallas as pl
from jax.experimental.pallas import tpu as pltpu
from jax.sharding import PartitionSpec as P

HD = 128
SIDE = 4
ROWS = 256
CODE_ROWS = 16
CLIP_STEP = 8192
MESH = pl.DeviceIdType.MESH
NT = (((1,), (1,)), ((), ()))
TN = (((0,), (0,)), ((), ()))
NN = (((1,), (0,)), ((), ()))
f32 = jnp.float32
bf16 = jnp.bfloat16
highest = lax.Precision.HIGHEST
VMEM_LIMIT = 60 << 20
HOPS = (1, 3, 2)


def dot(lhs, rhs, dims=NN):
    return lax.dot_general(lhs, rhs, dims, preferred_element_type=f32)


def place():
    tok = lax.axis_index("tok")
    return (lax.div(tok, 8), lax.axis_index("head"), lax.rem(lax.div(tok, 2), 4), lax.rem(tok, 2))


def around(index, step):
    return lax.rem(index + (step % SIDE), SIDE)


def device(x, y, z, core):
    return (x * 8 + z * 2 + core, y)


def remote(src, dst, send_sem, recv_sem, target):
    return pltpu.make_async_remote_copy(
        src_ref=src,
        dst_ref=dst,
        send_sem=send_sem,
        recv_sem=recv_sem,
        device_id=target,
        device_id_type=MESH,
    )


def greet(targets):
    barrier = pltpu.get_barrier_semaphore()
    for target in targets:
        pl.semaphore_signal(barrier, inc=1, device_id=target, device_id_type=MESH)
    return lambda: pl.semaphore_wait(barrier, len(targets))


class Copies:
    def __init__(self, send_sems, recv_sems):
        self.send_sems = send_sems
        self.recv_sems = recv_sems
        self.used = 0
        self.open = []

    def start(self, src, dst, target, landing):
        index = self.used
        self.used += 1
        copy = remote(src, dst, self.send_sems.at[index], self.recv_sems.at[index], target)
        copy.start()
        self.open.append(copy)
        return remote(landing, landing, self.send_sems.at[index], self.recv_sems.at[index], target)

    def finish(self):
        for copy in self.open:
            copy.wait_send()


def sum_over_y(copies, here, given, came, total):
    x, y, z, core = here
    arrivals = []
    for n, hop in enumerate(HOPS):
        other = around(y, hop)
        arrivals.append(
            copies.start(given.at[other], came.at[n], device(x, other, z, core), came.at[n])
        )
    yield
    for arrival in arrivals:
        arrival.wait_recv()
    total[y] = (
        (given[y].astype(f32) + came[0].astype(f32))
        + (came[1].astype(f32) + came[2].astype(f32))
    ).astype(bf16)
    arrivals = []
    for hop in HOPS:
        arrivals.append(
            copies.start(
                total.at[y],
                total.at[y],
                device(x, around(y, hop), z, core),
                total.at[around(y, -hop)],
            )
        )
    yield
    for arrival in arrivals:
        arrival.wait_recv()
    yield


def sum_scratch(width):
    quarter = ROWS // SIDE
    return [
        pltpu.VMEM((2, 3, quarter, width // 2), bf16),
        pltpu.VMEM((2, SIDE, quarter, width // 2), bf16),
        pltpu.SemaphoreType.DMA((12,)),
        pltpu.SemaphoreType.DMA((12,)),
    ]


def summed_rows(all_rows, index):
    part = lax.div(index, SIDE // 2)
    start = pl.multiple_of(lax.rem(index, SIDE // 2) * NORM_ROWS, NORM_ROWS)
    halves = [all_rows[half, part, pl.ds(start, NORM_ROWS), :] for half in range(2)]
    return jnp.concatenate(halves, axis=1).astype(f32)


def ring_sum(copies, own, towards, block, slots):
    up, down = towards(1), towards(-1)
    from_down = copies.start(block(2, 0), slots.at[0], up, slots.at[0])
    from_up = copies.start(block(2, 1), slots.at[1], down, slots.at[1])
    raw_down = copies.start(block(1, 1), slots.at[2], up, slots.at[2])
    raw_up = copies.start(block(-1, 0), slots.at[3], down, slots.at[3])
    yield
    from_down.wait_recv()
    onward = block(1, 0)
    onward[...] = (onward[...].astype(f32) + slots[0].astype(f32)).astype(bf16)
    sum_down = copies.start(onward, slots.at[4], up, slots.at[4])
    from_up.wait_recv()
    onward = block(-1, 1)
    onward[...] = (onward[...].astype(f32) + slots[1].astype(f32)).astype(bf16)
    sum_up = copies.start(onward, slots.at[5], down, slots.at[5])
    yield
    for arrival in (raw_down, raw_up, sum_down, sum_up):
        arrival.wait_recv()

    def finished(half):
        mine = block(0, half)[...].astype(f32)
        if half == 0:
            return mine + slots[4].astype(f32) + slots[3].astype(f32)
        return mine + slots[2].astype(f32) + slots[5].astype(f32)

    own.append(finished)


def ring_shapes(rows, cols):
    if rows >= 32:
        width = cols // 4
        return 2, (2 * rows, width), (rows // 2, width)
    return 1, (4 * rows, cols // 4), (rows, cols // 4)


def weight_scratch(rows, cols):
    chunks, first, late = ring_shapes(rows, cols)
    return [
        pltpu.VMEM((16, rows, 2 * ROWS), bf16),
        pltpu.VMEM((2 * ROWS, cols), bf16),
        pltpu.VMEM((2, chunks, 4, 2) + first, bf16),
        pltpu.VMEM((2, chunks, 6) + first, bf16),
        pltpu.VMEM((2, chunks, 4, 2) + late, bf16),
        pltpu.VMEM((2, chunks, 6) + late, bf16),
        pltpu.SemaphoreType.DMA((2 + 24 * chunks,)),
        pltpu.SemaphoreType.DMA((2 + 24 * chunks,)),
        pltpu.SemaphoreType.DMA((2,)),
    ]


def store_part(out, row, start, value):
    rows = slice(row, row + value.shape[0])
    if len(out.shape) == 2:
        out[rows, start : start + value.shape[1]] = value
        return
    size, done = out.shape[2], 0
    while done < value.shape[1]:
        block, offset = divmod(start + done, size)
        count = min(size - offset, value.shape[1] - done)
        out[block, rows, offset : offset + count] = value[:, done : done + count]
        done += count


def pick(core_at, factor, rows, group):
    row = lax.broadcasted_iota(jnp.int32, (256, 512), 0)
    col = lax.broadcasted_iota(jnp.int32, (256, 512), 1)
    wanted = lax.div(row, rows) * (2 * rows) + core_at * rows + lax.rem(row, rows)
    chosen = jnp.where(col == wanted, 1.0, 0.0).astype(bf16)
    return dot(chosen, factor[:, 512 * group : 512 * (group + 1)], NT).astype(bf16)


def weight_grad(here, left, right, out, scratch, far=None):
    both_left, both_right, parts, came, sums, late, send_sems, recv_sems, own_sems = scratch
    x, y, z, core = here
    rows, cols = both_left.shape[1], both_right.shape[1]
    copies = Copies(send_sems, recv_sems)
    twin = device(x, y, z, 1 - core)
    if far is None:
        far = left.at[:, 1 - core]
        own_left = pltpu.make_async_copy(
            left.at[:, core], both_left.at[:, :, pl.ds(0, ROWS)], own_sems.at[0]
        )
        own_right = pltpu.make_async_copy(right, both_right.at[pl.ds(0, ROWS)], own_sems.at[1])
        own_left.start()
        own_right.start()
    else:
        right = both_right.at[pl.ds(0, ROWS)]
        own_left = own_right = None
    far_left = copies.start(
        far,
        both_left.at[:, :, pl.ds(ROWS, ROWS)],
        twin,
        both_left.at[:, :, pl.ds(ROWS, ROWS)],
    )
    far_right = copies.start(
        right,
        both_right.at[pl.ds(ROWS, ROWS)],
        twin,
        both_right.at[pl.ds(ROWS, ROWS)],
    )
    yield
    if own_left is not None:
        own_left.wait()
        own_right.wait()
    far_left.wait_recv()
    far_right.wait_recv()

    chunks, first_shape, late_shape = ring_shapes(rows, cols)
    by_rows = chunks == 2
    width = cols // 2 // chunks

    def spot(way, step):
        return around(x if way == 0 else z, step)

    def fill(way, chunk, step):
        at = spot(way, step)
        if way == 0:
            chosen = both_left[pl.ds(at * 4, 4)].reshape(4 * rows, 2 * ROWS)
        else:
            chosen = jnp.concatenate([both_left[k * 4 + at] for k in range(4)], axis=0)
        start = (way * chunks + chunk) * width
        value = dot(chosen, both_right[:, start : start + width]).astype(bf16)
        if by_rows:
            parts[way, chunk, at] = value.reshape((2,) + first_shape)
        else:
            for half_index in range(2):
                parts[way, chunk, at, half_index] = value[
                    :, half_index * first_shape[1] : (half_index + 1) * first_shape[1]
                ]

    def towards(way):
        def target(step):
            if way == 0:
                return device(around(x, step), y, z, core)
            return device(x, y, around(z, step), core)

        return target

    every = [(way, chunk) for chunk in range(chunks) for way in (0, 1)]
    first, first_done = {}, {}
    for way, chunk in every:
        for step in (2, 1, -1):
            fill(way, chunk, step)
        first_done[way, chunk] = []
        first[way, chunk] = ring_sum(
            copies,
            first_done[way, chunk],
            towards(way),
            lambda step, half_index, way=way, chunk=chunk: parts.at[
                way, chunk, spot(way, step), half_index
            ],
            came.at[way, chunk],
        )
        next(first[way, chunk])
    for way, chunk in every:
        fill(way, chunk, 0)
    yield
    for chunk in range(2):
        for way in (0, 1):
            if chunk < chunks:
                next(first[way, chunk])
        yield
    second, second_done = {}, {}
    for chunk in range(2):
        for way in (0, 1):
            if chunk >= chunks:
                continue
            next(first[way, chunk], None)
            finished = first_done[way, chunk][0]
            for half_index in (0, 1):
                value = finished(half_index).astype(bf16)
                if by_rows:
                    sums[way, chunk, 2 * half_index : 2 * half_index + 2] = value.reshape(
                        (2, 2) + late_shape
                    )
                else:
                    sums[way, chunk, :, half_index] = value.reshape((4,) + late_shape)
            second_done[way, chunk] = []
            second[way, chunk] = ring_sum(
                copies,
                second_done[way, chunk],
                towards(1 - way),
                lambda step, half_index, way=way, chunk=chunk: sums.at[
                    way, chunk, spot(1 - way, step), half_index
                ],
                late.at[way, chunk],
            )
            next(second[way, chunk])
        yield
    for at in every:
        next(second[at])
    yield
    for way, chunk in every:
        next(second[way, chunk], None)
        start = (way * chunks + chunk) * width
        for half_index in (0, 1):
            value = second_done[way, chunk][0](half_index)
            if by_rows:
                store_part(out, half_index * late_shape[0], start, value)
            else:
                store_part(out, 0, start + half_index * late_shape[1], value)
    copies.finish()
    yield


def sum_gains(copies, here, given, came_x, part_x, came_z, part_z, came_core, part, came_y, out):
    x, y, z, core = here
    arrivals = [
        copies.start(
            given.at[around(x, hop)], came_x.at[n], device(around(x, hop), y, z, core), came_x.at[n]
        )
        for n, hop in enumerate(HOPS)
    ]
    yield
    for arrival in arrivals:
        arrival.wait_recv()
    part_x[...] = (given[x] + came_x[0]) + (came_x[1] + came_x[2])
    arrivals = [
        copies.start(
            part_x.at[around(z, hop)], came_z.at[n], device(x, y, around(z, hop), core), came_z.at[n]
        )
        for n, hop in enumerate(HOPS)
    ]
    yield
    for arrival in arrivals:
        arrival.wait_recv()
    part_z[...] = (part_x[z] + came_z[0]) + (came_z[1] + came_z[2])
    arrival = copies.start(part_z.at[1 - core], came_core, device(x, y, z, 1 - core), came_core)
    yield
    arrival.wait_recv()
    part[...] = part_z[core] + came_core[...]
    arrivals = [
        copies.start(part, came_y.at[n], device(x, around(y, hop), z, core), came_y.at[n])
        for n, hop in enumerate(HOPS)
    ]
    yield
    for arrival in arrivals:
        arrival.wait_recv()
    out[...] = (part[...] + came_y[0]) + (came_y[1] + came_y[2])
    yield


GAIN_SCRATCH = [(3, 4, 2, 8, HD), (4, 2, 8, HD), (3, 2, 8, HD), (2, 8, HD), (8, HD), (8, HD), (3, 8, HD)]


NORM_ROWS = 32
WIDE = 512


def gain_rows(labels, gains, first):
    return jnp.where(
        labels == 0,
        gains[first : first + 1, :],
        jnp.where(labels == 1, gains[first + 1 : first + 2, :], gains[first + 2 : first + 3, :]),
    )


def steps(count, body):
    lax.fori_loop(0, count, lambda index, carry: (body(index), carry)[1], 0)


def slab(index, size):
    return pl.ds(pl.multiple_of(index * size, size), size)


def visible(key_codes, low, span):
    return (key_codes - low).astype(jnp.uint32) <= span.astype(jnp.uint32)


def key_column(keys_values, z_at, core_at):
    codes = jnp.concatenate(
        [keys_values[z_at, core_at, n, ROWS:, :] for n in range(4)], axis=1
    )
    row = lax.broadcasted_iota(jnp.int32, (CODE_ROWS, HD), 0)
    weight = jnp.where(row == 0, 128.0, jnp.where(row == 1, 1.0, 0.0)).astype(bf16)
    return dot(codes, weight, TN).astype(jnp.int32)


def query_bounds(keys_values, z, core, bounds):
    for n in range(4):
        digits = keys_values[z, core, n, ROWS:, :].astype(f32)
        code = (digits[0:1] * 128.0 + digits[1:2]).astype(jnp.int32)
        low = jnp.where(code >= CLIP_STEP, CLIP_STEP, 0)
        bounds[0:1, n * ROWS : (n + 1) * ROWS] = low
        bounds[1:2, n * ROWS : (n + 1) * ROWS] = code - low


def forward_kernel(
    x_ref, label_ref, position_ref, gains_ref, cotangent_ref, weight_hbm, out_weight_hbm, down_hbm,
    q_all_ref, kv_all_ref, o_ref, lse_ref, returned_ref, total_ref, grad_active_hbm, weights_ref, tops_ref, labels_ref,
    cos_ref, sin_ref,
    grad_active_ref, weight, out_weight, down, weights, normed, q_own, kv_own, queries, keys_values, top, norm, acc, column, bounds_ref, o_low, back,
    gathered, send_sems, recv_sems, load_sems, weight_sems,
):
    here = place()
    x, y, z, core = here
    twin = device(x, y, z, 1 - core)
    arrived = greet(
        [device(around(x, hop), y, z, core) for hop in HOPS]
        + [device(x, around(y, hop), z, core) for hop in HOPS]
        + [device(x, y, around(z, hop), core) for hop in (1, 3)]
        + [twin]
    )
    load_out = pltpu.make_async_copy(out_weight_hbm, out_weight.at[y], load_sems.at[0])
    load_out.start()
    load = pltpu.make_async_copy(weight_hbm, weight, load_sems.at[1])
    load.start()
    load_down = pltpu.make_async_copy(down_hbm, down, load_sems.at[3])
    load_down.start()
    copies = Copies(send_sems, recv_sems)

    position = position_ref[...]
    block, row = lax.shift_right_logical(position, 8), lax.bitwise_and(position, 255)
    second = row >= 192
    spot = jnp.where(second, block * 64 + row - 192, block * 192 + row)
    code = spot + jnp.where(second, CLIP_STEP, 0)
    kind = lax.broadcasted_iota(jnp.int32, (CODE_ROWS, ROWS), 0)
    digits = jnp.where(
        kind == 0,
        lax.shift_right_logical(code, 7),
        jnp.where(kind == 1, lax.bitwise_and(code, 127), 0),
    )
    digits = digits.astype(f32).astype(bf16)
    kind = lax.broadcasted_iota(jnp.int32, (8, ROWS), 0)
    small = jnp.where(
        kind == 0,
        lax.shift_right_logical(spot, 7),
        jnp.where(kind == 1, lax.bitwise_and(spot, 127), jnp.where(kind == 2, label_ref[...], 0)),
    )
    small = small.astype(f32).astype(bf16)
    kind = lax.broadcasted_iota(jnp.int32, (8, HD), 0)
    spot_weight = jnp.where(kind == 0, 128.0, jnp.where(kind == 1, 1.0, 0.0)).astype(bf16)
    label_weight = jnp.where(kind == 2, 1.0, 0.0).astype(bf16)
    labels_ref[...] = dot(small, label_weight, TN).astype(jnp.int32)
    feature = lax.rem(lax.broadcasted_iota(jnp.int32, (1, HD), 1), HD // 2).astype(f32)
    angle = dot(small, spot_weight, TN) * jnp.exp(feature * (-2.0 * math.log(10000.0) / HD))
    cos_ref[...] = jnp.cos(angle)
    sin_ref[...] = jnp.sin(angle)

    def normalise(index):
        at = slab(index, NORM_ROWS)
        rows = x_ref[at, :].astype(f32)
        centred = rows - jnp.mean(rows, axis=-1, keepdims=True)
        scale = lax.rsqrt(jnp.mean(centred * centred, axis=-1, keepdims=True) + 1e-05)
        normed[at, :] = (centred * scale * gain_rows(labels_ref[at, :1], gains_ref, 0)).astype(
            bf16
        )

    steps(ROWS // NORM_ROWS, normalise)
    arrived()
    load_out.wait()
    y_up, y_down = device(x, around(y, 1), z, core), device(x, around(y, -1), z, core)
    y_next, y_last, y_far = around(y, 1), around(y, -1), around(y, 2)
    w_last, w_next, w_far, w_twin = [], [], [None] * 4, []
    for n in range(4):
        block = out_weight.at[y, core, n]
        w_last.append(copies.start(block, block, y_up, out_weight.at[y_last, core, n]))
        w_next.append(copies.start(block, block, y_down, out_weight.at[y_next, core, n]))

    def w_onward(n):
        w_last[n].wait_recv()
        block = out_weight.at[y_last, core, n]
        if n < 2:
            w_far[n] = copies.start(block, block, y_up, out_weight.at[y_far, core, n])
        w_twin.append(copies.start(block, block, twin, out_weight.at[y_last, 1 - core, n]))
        w_next[n].wait_recv()
        block = out_weight.at[y_next, core, n]
        if n >= 2:
            w_far[n] = copies.start(block, block, y_down, out_weight.at[y_far, core, n])
        w_twin.append(copies.start(block, block, twin, out_weight.at[y_next, 1 - core, n]))

    load.wait()
    cosine, sine = cos_ref[...], sin_ref[...]

    def rotate(values, head):
        part = values[:, head * HD : (head + 1) * HD]
        turned = jnp.concatenate([-part[:, HD // 2 :], part[:, : HD // 2]], axis=1)
        return part * cosine + turned * sine

    key_part = dot(normed[...], weight[1])
    for head in range(4):
        kv_own[head, :ROWS, :HD] = rotate(key_part, head).astype(bf16)
        kv_own[head, ROWS:, :] = digits
    value_part = dot(normed[...], weight[2])
    for head in range(4):
        kv_own[head, :ROWS, HD:] = value_part[:, head * HD : (head + 1) * HD].astype(bf16)
    kv_came, q_came = [None] * 3, [None] * 3

    def send_kv(n):
        other = around(x, HOPS[n])
        kv_came[n] = copies.start(
            kv_own.at[other],
            keys_values.at[z, core, x],
            device(other, y, z, core),
            keys_values.at[z, core, around(x, -HOPS[n])],
        )

    send_kv(0)
    send_kv(1)
    query_part = dot(normed[...], weight[0]) * (HD**-0.5 / math.log(2.0))
    for head in range(4):
        q_own[head] = rotate(query_part, head).astype(bf16)
    for n, hop in enumerate(HOPS):
        other = around(x, hop)
        q_came[n] = copies.start(
            q_own.at[other],
            queries.at[x],
            device(other, y, z, core),
            queries.at[around(x, -hop)],
        )
    send_kv(2)
    keys_values[z, core, x] = kv_own[x]
    queries[x] = q_own[x]
    above, below = device(x, y, around(z, 1), core), device(x, y, around(z, -1), core)
    next_z, last_z, far_z = around(z, 1), around(z, -1), around(z, 2)
    pieces = [x] + [around(x, -hop) for hop in HOPS]
    from_last, from_next, from_twin = [], [], []

    def spread(n):
        block = keys_values.at[z, core, pieces[n]]
        from_last.append(copies.start(block, block, above, keys_values.at[last_z, core, pieces[n]]))
        from_next.append(copies.start(block, block, below, keys_values.at[next_z, core, pieces[n]]))
        from_twin.append(copies.start(block, block, twin, keys_values.at[z, 1 - core, pieces[n]]))

    spread(0)
    top[...] = jnp.full_like(top, -1e30)
    norm[...] = jnp.zeros_like(norm)
    acc[...] = jnp.zeros_like(acc)
    load_down.wait()

    def grad_active(index):
        at = slab(index, WIDE)
        grad_active_ref[:, at] = dot(cotangent_ref[...], down[at, :], NT)

    half_steps = grad_active_ref.shape[1] // WIDE // 2
    keep_grad = pltpu.make_async_copy(grad_active_ref, grad_active_hbm, load_sems.at[4])
    steps(half_steps, grad_active)
    for n in range(3):
        kv_came[n].wait_recv()
        spread(n + 1)
        if n == 1:
            steps(half_steps, lambda index: grad_active(index + half_steps))
            keep_grad.start()
    for arrival in q_came:
        arrival.wait_recv()
    query_bounds(keys_values, z, core, bounds_ref)

    stored = []

    def attend(z_at, core_at):
        count = len(stored)
        column[...] = key_column(keys_values, z_at, core_at)
        query = queries[...].reshape(4 * ROWS, HD)
        keys = keys_values[z_at, core_at, :, :ROWS, :HD].reshape(4 * ROWS, HD)
        values = keys_values[z_at, core_at, :, :ROWS, HD:].reshape(4 * ROWS, HD)
        scores = dot(keys, query, NT)
        codes = jnp.concatenate([column[...]] * (4 * ROWS // HD), axis=1)
        seen = visible(codes, bounds_ref[0:1, :], bounds_ref[1:2, :])
        scores = jnp.where(seen, scores, -1e30)
        top_before = top[0:1, :]
        top_now = jnp.maximum(top_before, jnp.max(scores, axis=0, keepdims=True))
        if count >= 2:
            stored[count - 2].wait()
        slot = weights.at[count % 2]
        slot[...] = jnp.exp2(scores - top_now).astype(bf16)
        shrink = jnp.exp2(top_before - top_now)
        norm[...] = norm[...] * shrink + dot(jnp.ones((8, 4 * ROWS), bf16), slot[...])
        top[0:1, :] = top_now
        acc[...] = acc[...] * shrink + dot(values, slot[...], TN)
        tops_ref[z_at, core_at] = jnp.broadcast_to(top_now, tops_ref.shape[2:])
        copy = pltpu.make_async_copy(
            slot, weights_ref.at[z_at, core_at], weight_sems.at[count % 2]
        )
        copy.start()
        stored.append(copy)

    low_far, high_far, twin_last, twin_next = [], [], [], []

    def onward(n):
        piece = pieces[n]
        from_last[n].wait_recv()
        block = keys_values.at[last_z, core, piece]
        low = block.at[pl.ds(0, ROWS // 2)]
        low_far.append(
            copies.start(low, low, above, keys_values.at[far_z, core, piece, pl.ds(0, ROWS // 2)])
        )
        twin_last.append(
            copies.start(block, block, twin, keys_values.at[last_z, 1 - core, piece])
        )
        from_next[n].wait_recv()
        block = keys_values.at[next_z, core, piece]
        high = block.at[pl.ds(ROWS // 2, ROWS // 2 + CODE_ROWS)]
        high_far.append(
            copies.start(
                high,
                high,
                below,
                keys_values.at[far_z, core, piece, pl.ds(ROWS // 2, ROWS // 2 + CODE_ROWS)],
            )
        )
        twin_next.append(
            copies.start(block, block, twin, keys_values.at[next_z, 1 - core, piece])
        )

    def take(arrivals):
        for arrival in arrivals:
            arrival.wait_recv()

    onward(0)
    w_onward(0)
    attend(z, core)
    onward(1)
    onward(2)
    take(from_twin)
    attend(z, 1 - core)
    onward(3)
    w_onward(1)
    attend(last_z, core)
    attend(next_z, core)
    w_onward(2)
    take(twin_last)
    attend(last_z, 1 - core)
    twin_far = []
    for n, piece in enumerate(pieces):
        low_far[n].wait_recv()
        high_far[n].wait_recv()
        block = keys_values.at[far_z, core, piece]
        twin_far.append(copies.start(block, block, twin, keys_values.at[far_z, 1 - core, piece]))
    take(twin_next)
    attend(next_z, 1 - core)
    w_onward(3)
    attend(far_z, core)
    take(twin_far)
    keep = pltpu.make_async_copy(keys_values, kv_all_ref, load_sems.at[2])
    keep.start()
    attend(far_z, 1 - core)

    total_norm = norm[0:1, :]
    attended = (acc[...] / total_norm).T
    o_low[...] = attended.astype(bf16).reshape(4, ROWS, HD)
    came_back = []
    for hop in HOPS:
        other = around(x, hop)
        came_back.append(
            copies.start(
                o_low.at[other],
                back.at[x],
                device(other, y, z, core),
                back.at[around(x, -hop)],
            )
        )
    back[x] = o_low[x]
    o_ref[...] = attended
    lse_ref[...] = jnp.broadcast_to(top[0:1, :] + jnp.log2(total_norm), lse_ref.shape)
    q_all_ref[...] = queries[...]
    for n in range(4):
        w_far[n].wait_recv()
        block = out_weight.at[y_far, core, n]
        w_twin.append(copies.start(block, block, twin, out_weight.at[y_far, 1 - core, n]))
    take(came_back)
    local = 4 * HD
    mine = pl.ds(pl.multiple_of(y * local, local), local)
    for n in range(4):
        gathered[y, :, n * HD : (n + 1) * HD] = back[n]
    spread_y = [
        copies.start(
            gathered.at[y],
            gathered.at[y],
            device(x, around(y, hop), z, core),
            gathered.at[around(y, -hop)],
        )
        for hop in HOPS
    ]
    returned_ref[...] = gathered[y]
    take(w_twin)
    take(spread_y)

    def project(index):
        at = slab(index, WIDE)
        total_ref[:, at] = sum(
            dot(gathered[n], out_weight[n, :, :, :, at].reshape(local, WIDE)) for n in range(4)
        ).astype(bf16)

    steps(total_ref.shape[1] // WIDE, project)
    copies.finish()
    keep.wait()
    keep_grad.wait()
    for copy in stored[-2:]:
        copy.wait()


def attention_forward(
    activations, labels, position, gains, cotangent, weight, out_weight, down_weight
):
    width = out_weight.shape[1]
    whole = pl.BlockSpec(memory_space=pltpu.VMEM)
    anywhere = pl.BlockSpec(memory_space=pl.ANY)
    count = 3 + 3 + 12 + 16 + 4 + 3 + 3 + 8 + 4 + 8 + 4
    pieces = (2, 4, out_weight.shape[0] // 8, width)
    return pl.pallas_call(
        forward_kernel,
        out_shape=[
            jax.ShapeDtypeStruct((4, ROWS, HD), bf16),
            jax.ShapeDtypeStruct((4, 2, 4, ROWS + CODE_ROWS, 2 * HD), bf16),
            jax.ShapeDtypeStruct((4 * ROWS, HD), f32),
            jax.ShapeDtypeStruct((8, 4 * ROWS), f32),
            jax.ShapeDtypeStruct((ROWS, 4 * HD), bf16),
            jax.ShapeDtypeStruct((ROWS, width), bf16),
            jax.ShapeDtypeStruct((ROWS, down_weight.shape[0]), f32),
            jax.ShapeDtypeStruct((4, 2, 4 * ROWS, 4 * ROWS), bf16),
            jax.ShapeDtypeStruct((4, 2, 8, 4 * ROWS), f32),
            jax.ShapeDtypeStruct((ROWS, HD), jnp.int32),
            jax.ShapeDtypeStruct((ROWS, HD), f32),
            jax.ShapeDtypeStruct((ROWS, HD), f32),
        ],
        in_specs=[whole] * 5 + [anywhere] * 3,
        out_specs=[whole, anywhere] + [whole] * 4 + [anywhere, anywhere] + [whole] * 4,
        scratch_shapes=[
            pltpu.VMEM((ROWS, down_weight.shape[0]), f32),
            pltpu.VMEM(weight.shape, bf16),
            pltpu.VMEM((4,) + pieces, bf16),
            pltpu.VMEM(down_weight.shape, bf16),
            pltpu.VMEM((2, 4 * ROWS, 4 * ROWS), bf16),
            pltpu.VMEM(activations.shape, bf16),
            pltpu.VMEM((4, ROWS, HD), bf16),
            pltpu.VMEM((4, ROWS + CODE_ROWS, 2 * HD), bf16),
            pltpu.VMEM((4, ROWS, HD), bf16),
            pltpu.VMEM((4, 2, 4, ROWS + CODE_ROWS, 2 * HD), bf16),
            pltpu.VMEM((8, 4 * ROWS), f32),
            pltpu.VMEM((8, 4 * ROWS), f32),
            pltpu.VMEM((HD, 4 * ROWS), f32),
            pltpu.VMEM((4 * ROWS, HD), jnp.int32),
            pltpu.VMEM((8, 4 * ROWS), jnp.int32),
            pltpu.VMEM((4, ROWS, HD), bf16),
            pltpu.VMEM((4, ROWS, HD), bf16),
            pltpu.VMEM((4, ROWS, 4 * HD), bf16),
            pltpu.SemaphoreType.DMA((count,)),
            pltpu.SemaphoreType.DMA((count,)),
            pltpu.SemaphoreType.DMA((5,)),
            pltpu.SemaphoreType.DMA((2,)),
        ],
        compiler_params=pltpu.CompilerParams(
            collective_id=0, has_side_effects=True, vmem_limit_bytes=VMEM_LIMIT
        ),
        name="attention_forward",
    )(
        activations,
        labels,
        position,
        gains,
        cotangent,
        weight,
        out_weight.reshape(pieces),
        down_weight,
    )


def gelu_and_slope(hidden):
    scale = math.sqrt(2.0 / math.pi)
    square = hidden * hidden
    bent = jnp.tanh(scale * hidden * (1.0 + 0.044715 * square))
    half = 0.5 * (1.0 + bent)
    slope = half + 0.5 * hidden * (1.0 - bent * bent) * (scale * (1.0 + 3 * 0.044715 * square))
    return hidden * half, slope


def middle_kernel(
    x_ref, attn_ref, labels_ref, gains_ref, cotangent_hbm, out_weight_hbm, grad_active_hbm, up_hbm, down_hbm,
    g_mid_hbm, g_low_hbm, heads_ref, mlp_hbm, active_left_hbm, gains_out_ref, grad_up_ref, grad_down_ref,
    up, down, cotangent, out_weight, grad_active, g_mid, g_low, mlp, active_left, xhat, inverse, normed, active,
    far, far_down, given, g_heads, came, all_rows, y_send, y_recv, load_sems, x_send, x_recv, *more,
):
    here = place()
    x, y, z, core = here
    arrived = greet(
        [device(x, around(y, hop), z, core) for hop in HOPS]
        + [device(around(x, hop), y, z, core) for hop in HOPS]
        + [device(x, y, around(z, hop), core) for hop in (1, 3)]
        + [device(x, y, z, 1 - core)]
    )
    up_scratch, down_scratch = more[:9], more[9:]
    both_left, both_right = up_scratch[:2]
    down_left, down_right = down_scratch[:2]
    used = [0]

    def move(src, dst):
        copy = pltpu.make_async_copy(src, dst, load_sems.at[used[0]])
        used[0] += 1
        copy.start()
        return copy

    load_up = move(up_hbm, up)
    load_active = move(grad_active_hbm, grad_active)
    load_part = move(
        cotangent_hbm.at[:, pl.ds(0, down_right.shape[1])], down_right.at[pl.ds(0, ROWS)]
    )
    load_down = move(down_hbm, down)
    load_cotangent = move(cotangent_hbm, cotangent)
    load_out = move(out_weight_hbm, out_weight)
    width = x_ref.shape[1]
    hidden_width = up.shape[1]

    def norm(index):
        at = slab(index, NORM_ROWS)
        middle = x_ref[at, :].astype(f32) + attn_ref[at, :].astype(f32)
        centred = middle - jnp.mean(middle, axis=-1, keepdims=True)
        scale = lax.rsqrt(jnp.mean(centred * centred, axis=-1, keepdims=True) + 1e-05)
        unit = centred * scale
        xhat[at, :] = unit
        inverse[at, :] = jnp.broadcast_to(scale, (NORM_ROWS, HD))
        normed[at, :] = (unit * gain_rows(labels_ref[at, :1], gains_ref, 3)).astype(bf16)

    steps(ROWS // NORM_ROWS, norm)
    rows = grad_up_ref.shape[0]
    for group in range(4):
        at = pl.ds(4 * group, 4)
        both_left[at, :, pl.ds(0, ROWS)] = pick(core, normed, rows, group).reshape(4, rows, ROWS)
        far[at] = pick(1 - core, normed, rows, group).reshape(4, rows, ROWS)
    load_up.wait()
    load_active.wait()

    def feed(index):
        at = slab(index, WIDE)
        hidden = dot(normed[...], up[:, at])
        value, slope = gelu_and_slope(hidden)
        active[:, at] = value.astype(bf16)
        both_right[pl.ds(0, ROWS), at] = (grad_active[:, at] * slope).astype(bf16)

    steps(hidden_width // WIDE, feed)
    arrived()
    ring = weight_grad(here, None, None, grad_up_ref, up_scratch, far)
    next(ring)

    copies = Copies(y_send, y_recv)
    half_steps = width // WIDE // 2
    over_y = []
    for half in range(2):

        def back_up(index, half=half):
            at = slab(index + half * half_steps, WIDE)
            part = dot(both_right[pl.ds(0, ROWS), :], up[at, :], NT)
            given[half, :, :, slab(index, WIDE)] = part.astype(bf16).reshape(
                SIDE, ROWS // SIDE, WIDE
            )

        steps(half_steps, back_up)
        over_y.append(
            sum_over_y(copies, here, given.at[half], came.at[half], all_rows.at[half])
        )
        next(over_y[half])
    next(ring)
    for group in range(4):
        at = pl.ds(4 * group, 4)
        for core_at in range(2):
            active_left[at, core_at] = pick(core_at, active, rows, group).reshape(4, rows, ROWS)
        down_left[at, :, pl.ds(0, ROWS)] = active_left[at, core]
        far_down[at] = active_left[at, 1 - core]
    load_part.wait()
    keep = [move(active_left, active_left_hbm)]
    ring_down = weight_grad(here, None, None, grad_down_ref, down_scratch, far_down)
    next(ring_down)
    load_down.wait()

    def feed_out(index, half):
        at = slab(index + half * half_steps, WIDE)
        mlp[half, :, :, slab(index, WIDE)] = (
            dot(active[...], down[:, at]).astype(bf16).reshape(SIDE, ROWS // SIDE, WIDE)
        )

    steps(half_steps, lambda index: feed_out(index, 0))
    next(over_y[0])
    next(ring_down)
    steps(half_steps, lambda index: feed_out(index, 1))
    keep.append(move(mlp, mlp_hbm))
    next(over_y[1])
    next(ring)
    next(ring)
    load_cotangent.wait()
    load_out.wait()
    gains_out_ref[...] = jnp.zeros_like(gains_out_ref)
    next(over_y[0])
    next(ring_down)
    next(ring)
    next(over_y[1])

    def back(index):
        at = slab(index, NORM_ROWS)
        grad = summed_rows(all_rows, index)
        labels = labels_ref[at, :1]
        unit = xhat[at, :]
        product = grad * unit
        for mode in range(3):
            gains_out_ref[mode + 3 : mode + 4, :] += jnp.sum(
                jnp.where(labels == mode, product, 0.0), axis=0, keepdims=True
            )
        gain = gain_rows(labels, gains_ref, 3)
        grad = grad * gain
        mean = jnp.mean(grad, axis=-1, keepdims=True)
        along = jnp.mean(product * gain, axis=-1, keepdims=True)
        total = cotangent[at, :].astype(f32) + inverse[at, :1] * (grad - mean - unit * along)
        g_mid[at, :] = total
        g_low[at, :] = total.astype(bf16)

    steps(ROWS // NORM_ROWS, back)
    by_head = dot(g_low[...], out_weight[...], NT).astype(bf16)
    for head in range(4):
        g_heads[head] = by_head[:, head * HD : (head + 1) * HD]
    x_copies = Copies(x_send, x_recv)
    arrivals = [
        x_copies.start(
            g_heads.at[around(x, hop)],
            heads_ref.at[x],
            device(around(x, hop), y, z, core),
            heads_ref.at[around(x, -hop)],
        )
        for hop in HOPS
    ]
    heads_ref[x] = g_heads[x]
    keep += [move(g_mid, g_mid_hbm), move(g_low, g_low_hbm)]
    next(ring_down)
    next(ring)
    next(ring_down)
    next(ring)
    next(ring_down)
    for arrival in arrivals:
        arrival.wait_recv()
    next(ring)
    next(ring_down)
    next(ring_down)
    copies.finish()
    x_copies.finish()
    for copy in keep:
        copy.wait()


def middle(
    activations, attn_sum, labels, gains, cotangent, out_weight, grad_active, up_weight, down_weight
):
    width, hidden_width = up_weight.shape
    rows = width // 32
    down_rows = hidden_width // 32
    whole = pl.BlockSpec(memory_space=pltpu.VMEM)
    anywhere = pl.BlockSpec(memory_space=pl.ANY)
    summed = (2, SIDE, ROWS // SIDE, width // 2)
    left = (16, 2, down_rows, ROWS)
    return pl.pallas_call(
        middle_kernel,
        out_shape=[
            jax.ShapeDtypeStruct((ROWS, width), f32),
            jax.ShapeDtypeStruct((ROWS, width), bf16),
            jax.ShapeDtypeStruct((4, ROWS, HD), bf16),
            jax.ShapeDtypeStruct(summed, bf16),
            jax.ShapeDtypeStruct(left, bf16),
            jax.ShapeDtypeStruct((8, width), f32),
            jax.ShapeDtypeStruct((rows, hidden_width), f32),
            jax.ShapeDtypeStruct((down_rows, width // 2), f32),
        ],
        in_specs=[whole] * 4 + [anywhere] * 5,
        out_specs=[anywhere] * 2 + [whole] + [anywhere] * 2 + [whole] * 3,
        scratch_shapes=[
            pltpu.VMEM(up_weight.shape, bf16),
            pltpu.VMEM(down_weight.shape, bf16),
            pltpu.VMEM((ROWS, width), bf16),
            pltpu.VMEM(out_weight.shape, bf16),
            pltpu.VMEM((ROWS, hidden_width), f32),
            pltpu.VMEM((ROWS, width), f32),
            pltpu.VMEM((ROWS, width), bf16),
            pltpu.VMEM(summed, bf16),
            pltpu.VMEM(left, bf16),
            pltpu.VMEM((ROWS, width), f32),
            pltpu.VMEM((ROWS, HD), f32),
            pltpu.VMEM((ROWS, width), bf16),
            pltpu.VMEM((ROWS, hidden_width), bf16),
            pltpu.VMEM((16, rows, ROWS), bf16),
            pltpu.VMEM((16, down_rows, ROWS), bf16),
            pltpu.VMEM(summed, bf16),
            pltpu.VMEM((4, ROWS, HD), bf16),
        ]
        + sum_scratch(width)
        + [pltpu.SemaphoreType.DMA((10,))]
        + [pltpu.SemaphoreType.DMA((3,)), pltpu.SemaphoreType.DMA((3,))]
        + weight_scratch(rows, hidden_width)
        + weight_scratch(down_rows, width // 2),
        compiler_params=pltpu.CompilerParams(
            collective_id=2, has_side_effects=True, vmem_limit_bytes=VMEM_LIMIT
        ),
        name="middle",
    )(
        activations,
        attn_sum,
        labels,
        gains,
        cotangent,
        out_weight,
        grad_active,
        up_weight,
        down_weight,
    )


def backward_kernel(
    grads, q_ref, kv_hbm, o_ref, lse_ref, tops_ref, weights_hbm, left_ref, right_ref, given_ref,
    packed_ref, weight_ref, total_ref,
    keys_values, weights, delta, grad_q, parts, met, came, sums, q_low, back_q,
    back_kv, send_sems, recv_sems, load_sems, weight_sems, y_came, all_rows, y_send, y_recv, *weight_scratch_refs,
):
    here = place()
    x, y, z, core = here
    twin = device(x, y, z, 1 - core)
    arrived = greet(
        [device(around(x, hop), y, z, core) for hop in HOPS]
        + [device(x, around(y, hop), z, core) for hop in HOPS]
        + [device(x, y, around(z, hop), core) for hop in (1, 3)]
        + [twin]
    )
    next_z, last_z, far_z = around(z, 1), around(z, -1), around(z, 2)
    order = [
        (at, core_at)
        for at in (far_z, next_z, last_z, z)
        for core_at in (1 - core, core)
    ]
    load = pltpu.make_async_copy(kv_hbm, keys_values, load_sems.at[0])
    load.start()

    def fetch(index):
        copy = pltpu.make_async_copy(
            weights_hbm.at[order[index][0], order[index][1]],
            weights.at[index % 3],
            weight_sems.at[index % 3],
        )
        copy.start()
        return copy

    fetched = [fetch(0), fetch(1)]
    copies = Copies(send_sems, recv_sems)
    y_copies = Copies(y_send, y_recv)
    over_y = [
        sum_over_y(y_copies, here, given_ref.at[half], y_came.at[half], all_rows.at[half])
        for half in range(2)
    ]
    half = weight_ref.shape[1]
    ring = weight_grad(
        here, left_ref, right_ref.at[:, pl.ds(half, half)], weight_ref, weight_scratch_refs
    )
    grad_q[...] = jnp.zeros_like(grad_q)
    product = grads[...].reshape(4 * ROWS, HD).astype(f32) * o_ref[...]
    delta[...] = lax.dot_general(
        jnp.ones((8, HD), f32), product, NT, preferred_element_type=f32, precision=highest
    )
    load.wait()
    arrived()
    next(ring)
    for half in over_y:
        next(half)
    done = []

    def chunk(z_at, core_at):
        index = len(done)
        done.append(index)
        if index + 2 < len(order):
            fetched.append(fetch(index + 2))
        fetched[index].wait()
        slot = weights.at[index % 3]
        query = q_ref[...].reshape(4 * ROWS, HD)
        grad = grads[...].reshape(4 * ROWS, HD)
        keys = keys_values[z_at, core_at, :, :ROWS, :HD].reshape(4 * ROWS, HD)
        values = keys_values[z_at, core_at, :, :ROWS, HD:].reshape(4 * ROWS, HD)
        rescale = jnp.exp2(tops_ref[z_at, core_at, 0:1, :] - lse_ref[0:1, :])
        grad_weights = dot(values, grad, NT)
        taken = slot[...].astype(f32) * rescale
        slot[...] = taken.astype(bf16)
        grad_v = dot(slot[...], grad)
        slot[...] = (taken * (grad_weights - delta[0:1, :])).astype(bf16)
        grad_k = dot(slot[...], query)
        grad_q[...] += dot(keys, slot[...], TN)
        parts[z_at, core_at] = (
            jnp.concatenate([grad_k * math.log(2.0), grad_v], axis=1)
            .astype(bf16)
            .reshape(2, 2 * ROWS, 2 * HD)
        )

    def hand_over(z_at):
        return copies.start(
            parts.at[z_at, 1 - core], met.at[z_at], twin, met.at[z_at]
        )

    def join(z_at):
        parts[z_at, core] = (
            parts[z_at, core].astype(f32) + met[z_at].astype(f32)
        ).astype(bf16)

    above, below = device(x, y, next_z, core), device(x, y, last_z, core)
    chunk(far_z, 1 - core)
    far_met = hand_over(far_z)
    next(ring)
    chunk(far_z, core)
    chunk(next_z, 1 - core)
    next_met = hand_over(next_z)
    far_met.wait_recv()
    join(far_z)
    from_last = copies.start(parts.at[far_z, core, 0], came.at[0], above, came.at[0])
    from_next = copies.start(parts.at[far_z, core, 1], came.at[1], below, came.at[1])
    chunk(next_z, core)
    next(ring)
    chunk(last_z, 1 - core)
    last_met = hand_over(last_z)
    next_met.wait_recv()
    join(next_z)
    raw_last = copies.start(parts.at[next_z, core, 1], came.at[2], above, came.at[2])
    for half in over_y:
        next(half)
    next(ring)
    chunk(last_z, core)
    chunk(z, 1 - core)
    own_met = hand_over(z)
    last_met.wait_recv()
    join(last_z)
    raw_next = copies.start(parts.at[last_z, core, 0], came.at[3], below, came.at[3])
    from_last.wait_recv()
    parts[next_z, core, 0] = (
        parts[next_z, core, 0].astype(f32) + came[0].astype(f32)
    ).astype(bf16)
    sum_last = copies.start(parts.at[next_z, core, 0], came.at[4], above, came.at[4])
    from_next.wait_recv()
    parts[last_z, core, 1] = (
        parts[last_z, core, 1].astype(f32) + came[1].astype(f32)
    ).astype(bf16)
    sum_next = copies.start(parts.at[last_z, core, 1], came.at[5], below, came.at[5])
    chunk(z, core)
    q_low[...] = (grad_q[...] * (HD**-0.5)).T.astype(bf16).reshape(4, ROWS, HD)
    arrivals = []
    for hop in HOPS:
        other = around(x, hop)
        arrivals.append(
            copies.start(
                q_low.at[other],
                back_q.at[x],
                device(other, y, z, core),
                back_q.at[around(x, -hop)],
            )
        )
    back_q[x] = q_low[x]
    next(ring)
    own_met.wait_recv()
    raw_last.wait_recv()
    raw_next.wait_recv()
    sum_last.wait_recv()
    sum_next.wait_recv()
    mine = parts[z, core].astype(f32) + met[z].astype(f32)
    low = mine[0] + came[4].astype(f32) + came[3].astype(f32)
    high = mine[1] + came[2].astype(f32) + came[5].astype(f32)
    sums[0:2] = low.astype(bf16).reshape(2, ROWS, 2 * HD)
    sums[2:4] = high.astype(bf16).reshape(2, ROWS, 2 * HD)
    for hop in HOPS:
        other = around(x, hop)
        arrivals.append(
            copies.start(
                sums.at[other],
                back_kv.at[x],
                device(other, y, z, core),
                back_kv.at[around(x, -hop)],
            )
        )
    back_kv[x] = sums[x]
    for half in over_y:
        next(half)
    total_ref[...] = all_rows[...]
    next(ring)
    next(ring)
    next(ring)
    for arrival in arrivals:
        arrival.wait_recv()
    for n in range(4):
        packed_ref[n, :, :HD] = back_q[n]
        packed_ref[n, :, HD:] = back_kv[n]
    copies.finish()
    y_copies.finish()


def attention_backward(grad_heads, q_all, kv_all, o_all, lse, tops, weights, left, right, given):
    whole = pl.BlockSpec(memory_space=pltpu.VMEM)
    anywhere = pl.BlockSpec(memory_space=pl.ANY)
    count = 4 + 6 + 6
    return pl.pallas_call(
        backward_kernel,
        out_shape=[
            jax.ShapeDtypeStruct((4, ROWS, 3 * HD), bf16),
            jax.ShapeDtypeStruct((left.shape[2], right.shape[1] // 2), f32),
            jax.ShapeDtypeStruct(given.shape, bf16),
        ],
        in_specs=[whole, whole, anywhere] + [whole] * 3 + [anywhere] * 3 + [whole],
        out_specs=[whole, whole, whole],
        scratch_shapes=[
            pltpu.VMEM((4, 2, 4, ROWS + CODE_ROWS, 2 * HD), bf16),
            pltpu.VMEM((3, 4 * ROWS, 4 * ROWS), bf16),
            pltpu.VMEM((8, 4 * ROWS), f32),
            pltpu.VMEM((HD, 4 * ROWS), f32),
            pltpu.VMEM((4, 2, 2, 2 * ROWS, 2 * HD), bf16),
            pltpu.VMEM((4, 2, 2 * ROWS, 2 * HD), bf16),
            pltpu.VMEM((6, 2 * ROWS, 2 * HD), bf16),
            pltpu.VMEM((4, ROWS, 2 * HD), bf16),
            pltpu.VMEM((4, ROWS, HD), bf16),
            pltpu.VMEM((4, ROWS, HD), bf16),
            pltpu.VMEM((4, ROWS, 2 * HD), bf16),
            pltpu.SemaphoreType.DMA((count,)),
            pltpu.SemaphoreType.DMA((count,)),
            pltpu.SemaphoreType.DMA((1,)),
            pltpu.SemaphoreType.DMA((3,)),
        ]
        + sum_scratch(2 * given.shape[3])
        + weight_scratch(left.shape[2], right.shape[1] // 2),
        compiler_params=pltpu.CompilerParams(
            collective_id=1, has_side_effects=True, vmem_limit_bytes=VMEM_LIMIT
        ),
        name="attention_backward",
    )(grad_heads, q_all, kv_all, o_all, lse, tops, weights, left, right, given)


def last_kernel(
    x_ref, labels_ref, gains_ref, returned_ref, packed_ref, cos_ref, sin_ref, gains_two_ref, g_low_hbm, attn_hbm,
    mlp_hbm, g_mid_hbm, weight_hbm,
    input_ref, layer_ref, gains_out_ref, grad_qkv_ref, grad_out_ref,
    attn, mlp, g_mid, weight, xhat, inverse, normed, far_qkv, far_out, given, gains_part, gains_given, came, all_rows, y_send, y_recv,
    load_sems, *more,
):
    gain_scratch = more[: len(GAIN_SCRATCH)]
    gain_send, gain_recv = more[len(GAIN_SCRATCH) : len(GAIN_SCRATCH) + 2]
    qkv_scratch = more[len(GAIN_SCRATCH) + 2 : len(GAIN_SCRATCH) + 11]
    out_scratch = more[len(GAIN_SCRATCH) + 11 :]
    here = place()
    x, y, z, core = here
    out_left, out_right = out_scratch[:2]
    loads = []
    for n, (src, dst) in enumerate(
        (
            (weight_hbm, weight),
            (g_low_hbm, out_right.at[pl.ds(0, ROWS)]),
            (attn_hbm, attn),
            (mlp_hbm, mlp),
            (g_mid_hbm, g_mid),
        )
    ):
        loads.append(pltpu.make_async_copy(src, dst, load_sems.at[n]))
        loads[n].start()
    arrived = greet(
        [device(x, around(y, hop), z, core) for hop in HOPS]
        + [device(around(x, hop), y, z, core) for hop in HOPS]
        + [device(x, y, around(z, hop), core) for hop in HOPS]
        + [device(x, y, z, 1 - core)]
    )
    width = x_ref.shape[1]
    local = returned_ref.shape[1]
    qkv_left, qkv_right = qkv_scratch[:2]
    qkv_rows, out_rows = grad_qkv_ref.shape[1], grad_out_ref.shape[0]

    cosine, sine = cos_ref[...], sin_ref[...]
    for head in range(4):
        for part in range(3):
            grad = packed_ref[head, :, part * HD : (part + 1) * HD]
            if part < 2:
                grad = grad.astype(f32)
                scaled = grad * sine
                grad = (
                    grad * cosine
                    + jnp.concatenate([scaled[:, HD // 2 :], -scaled[:, : HD // 2]], axis=1)
                ).astype(bf16)
            start = part * local + head * HD
            qkv_right[0:ROWS, start : start + HD] = grad

    def norm(index):
        at = slab(index, NORM_ROWS)
        rows = x_ref[at, :].astype(f32)
        centred = rows - jnp.mean(rows, axis=-1, keepdims=True)
        scale = lax.rsqrt(jnp.mean(centred * centred, axis=-1, keepdims=True) + 1e-05)
        unit = centred * scale
        xhat[at, :] = unit
        inverse[at, :] = jnp.broadcast_to(scale, (NORM_ROWS, HD))
        normed[at, :] = (unit * gain_rows(labels_ref[at, :1], gains_ref, 0)).astype(bf16)

    steps(ROWS // NORM_ROWS, norm)
    for group in range(4):
        at = pl.ds(4 * group, 4)
        qkv_left[at, :, pl.ds(0, ROWS)] = pick(core, normed, qkv_rows, group).reshape(
            4, qkv_rows, ROWS
        )
        far_qkv[at] = pick(1 - core, normed, qkv_rows, group).reshape(4, qkv_rows, ROWS)
    out_left[:, :, pl.ds(0, ROWS)] = pick(core, returned_ref, out_rows, 0).reshape(
        16, out_rows, ROWS
    )
    far_out[...] = pick(1 - core, returned_ref, out_rows, 0).reshape(16, out_rows, ROWS)
    arrived()
    rings = [
        weight_grad(here, None, None, grad_qkv_ref, qkv_scratch, far_qkv),
        weight_grad(here, None, None, grad_out_ref, out_scratch, far_out),
    ]
    loads[1].wait()
    for ring in rings:
        next(ring)
    loads[0].wait()
    gains_part[...] = 0.25 * gains_two_ref[...]
    copies = Copies(y_send, y_recv)
    half_steps = width // WIDE // 2
    over_y = []
    for half in range(2):

        def back_in(index, half=half):
            at = slab(index + half * half_steps, WIDE)
            part = sum(
                dot(qkv_right[pl.ds(0, ROWS), k * local : (k + 1) * local], weight[k, at, :], NT)
                for k in range(3)
            )
            given[half, :, :, slab(index, WIDE)] = part.astype(bf16).reshape(
                SIDE, ROWS // SIDE, WIDE
            )
            product = part * xhat[:, at]
            labels = labels_ref[:, :1]
            for mode in range(3):
                gains_part[mode : mode + 1, at] = jnp.sum(
                    jnp.where(labels == mode, product, 0.0), axis=0, keepdims=True
                )

        steps(half_steps, back_in)
        over_y.append(
            sum_over_y(copies, here, given.at[half], came.at[half], all_rows.at[half])
        )
        next(over_y[half])
    for owner in range(32):
        gains_given[owner // 8, (owner // 2) % 4, owner % 2] = jnp.zeros((8, HD), f32)
        gains_given[owner // 8, (owner // 2) % 4, owner % 2, :, :64] = gains_part[
            :, owner * 64 : (owner + 1) * 64
        ]
    gain_copies = Copies(gain_send, gain_recv)
    over_all = sum_gains(gain_copies, here, gains_given, *gain_scratch, gains_out_ref)
    next(over_all)
    for ring in rings:
        next(ring)
    for load in loads[2:]:
        load.wait()

    def finish_layer(index):
        at = slab(index, NORM_ROWS)
        total = x_ref[at, :].astype(f32) + attn[at, :].astype(f32) + summed_rows(mlp, index)
        layer_ref[at, :] = total.astype(bf16)

    steps(ROWS // NORM_ROWS, finish_layer)
    next(over_y[0])
    for ring in rings:
        next(ring)
    next(over_all)
    next(over_y[1])
    for step in range(2):
        for ring in rings:
            next(ring)
    next(over_y[0])
    for ring in rings:
        next(ring)
    next(over_all)
    next(over_y[1])

    def finish_input(index):
        at = slab(index, NORM_ROWS)
        unit = xhat[at, :]
        grad = summed_rows(all_rows, index) * gain_rows(labels_ref[at, :1], gains_ref, 0)
        mean = jnp.mean(grad, axis=-1, keepdims=True)
        along = jnp.mean(grad * unit, axis=-1, keepdims=True)
        input_ref[at, :] = g_mid[at, :] + inverse[at, :1] * (grad - mean - unit * along)

    steps(ROWS // NORM_ROWS, finish_input)
    for ring in rings:
        next(ring)
    next(over_all)
    for ring in rings:
        next(ring)
    next(over_all)
    copies.finish()
    gain_copies.finish()


def last(
    activations, labels, gains, returned, packed, cosine, sine, gains_two, g_low, attn_sum, mlp_sum, g_mid, weight
):
    width = activations.shape[1]
    local = returned.shape[1]
    cols = 3 * local
    rows = width // 32
    whole = pl.BlockSpec(memory_space=pltpu.VMEM)
    anywhere = pl.BlockSpec(memory_space=pl.ANY)
    return pl.pallas_call(
        last_kernel,
        out_shape=[
            jax.ShapeDtypeStruct((ROWS, width), f32),
            jax.ShapeDtypeStruct((ROWS, width), bf16),
            jax.ShapeDtypeStruct((8, HD), f32),
            jax.ShapeDtypeStruct((3, rows, local), f32),
            jax.ShapeDtypeStruct((local // 32, width), f32),
        ],
        in_specs=[whole] * 8 + [anywhere] * 5,
        out_specs=[whole] * 5,
        scratch_shapes=[
            pltpu.VMEM(attn_sum.shape, bf16),
            pltpu.VMEM(mlp_sum.shape, bf16),
            pltpu.VMEM(g_mid.shape, f32),
            pltpu.VMEM(weight.shape, bf16),
            pltpu.VMEM((ROWS, width), f32),
            pltpu.VMEM((ROWS, HD), f32),
            pltpu.VMEM((ROWS, width), bf16),
            pltpu.VMEM((16, rows, ROWS), bf16),
            pltpu.VMEM((16, local // 32, ROWS), bf16),
            pltpu.VMEM(mlp_sum.shape, bf16),
            pltpu.VMEM((8, width), f32),
            pltpu.VMEM((4, 4, 2, 8, HD), f32),
        ]
        + sum_scratch(width)
        + [pltpu.SemaphoreType.DMA((5,))]
        + [pltpu.VMEM(shape, f32) for shape in GAIN_SCRATCH]
        + [pltpu.SemaphoreType.DMA((10,)), pltpu.SemaphoreType.DMA((10,))]
        + weight_scratch(rows, cols)
        + weight_scratch(local // 32, width),
        compiler_params=pltpu.CompilerParams(
            collective_id=3, has_side_effects=True, vmem_limit_bytes=VMEM_LIMIT
        ),
        name="last",
    )(
        activations,
        labels,
        gains,
        returned,
        packed,
        cosine,
        sine,
        gains_two,
        g_low,
        attn_sum,
        mlp_sum,
        g_mid,
        weight,
    )


def finish_kernel(
    share_ref, layer_in, input_in, qkv_in, out_in, up_in, low_in, high_in,
    gains_ref, layer_out, input_out, qkv_out, out_out, up_out, down_out,
    layer, grad_input, qkv, out, up, low, high, load_sems, store_sems,
):
    half = low_in.shape[1]
    ways = (
        (layer_in, layer, layer_out),
        (up_in, up, up_out),
        (qkv_in, qkv, qkv_out),
        (low_in, low, down_out.at[:, pl.ds(0, half)]),
        (high_in, high, down_out.at[:, pl.ds(half, half)]),
        (out_in, out, out_out),
        (input_in, grad_input, input_out),
    )
    loads = [
        pltpu.make_async_copy(src, held, load_sems.at[n]) for n, (src, held, dst) in enumerate(ways)
    ]
    stores = [
        pltpu.make_async_copy(held, dst, store_sems.at[n]) for n, (src, held, dst) in enumerate(ways)
    ]
    for load in loads:
        load.start()
    gains_ref[...] = share_ref[: gains_ref.shape[0], : gains_ref.shape[1]]
    for load, store in zip(loads, stores):
        load.wait()
        store.start()
    for store in stores:
        store.wait()


def finish(modes, share, layer, grad_input, qkv, out, up, low, high):
    whole = pl.BlockSpec(memory_space=pltpu.VMEM)
    anywhere = pl.BlockSpec(memory_space=pl.ANY)
    results = [
        jax.ShapeDtypeStruct(array.shape, array.dtype) for array in (layer, grad_input, qkv, out, up)
    ]
    results.append(jax.ShapeDtypeStruct((low.shape[0], 2 * low.shape[1]), f32))
    return pl.pallas_call(
        finish_kernel,
        out_shape=[jax.ShapeDtypeStruct((2 * modes, layer.shape[1] // 32), f32)] + results,
        in_specs=[whole] + [anywhere] * 7,
        out_specs=[whole] + [anywhere] * 6,
        scratch_shapes=[
            pltpu.VMEM(array.shape, array.dtype)
            for array in (layer, grad_input, qkv, out, up, low, high)
        ]
        + [pltpu.SemaphoreType.DMA((7,)), pltpu.SemaphoreType.DMA((7,))],
        name="finish",
    )(share, layer, grad_input, qkv, out, up, low, high)


def per_device(
    activations,
    labels,
    position,
    norm_gains,
    qkv_weight,
    out_weight,
    up_weight,
    down_weight,
    cotangent,
):
    projections = qkv_weight.transpose(1, 0, 2)
    (
        q_all,
        kv_all,
        o_all,
        lse,
        returned,
        attn_sum,
        grad_active,
        weights,
        tops,
        label_rows,
        cosine,
        sine,
    ) = attention_forward(
        activations,
        labels.reshape(1, ROWS),
        position.reshape(1, ROWS),
        norm_gains,
        cotangent,
        projections,
        out_weight,
        down_weight,
    )
    g_mid, g_low, grad_heads, mlp_part, active_left, gains_two, grad_up, down_low = middle(
        activations,
        attn_sum,
        label_rows,
        norm_gains,
        cotangent,
        out_weight,
        grad_active,
        up_weight,
        down_weight,
    )
    packed, down_high, mlp_sum = attention_backward(
        grad_heads, q_all, kv_all, o_all, lse, tops, weights, active_left, cotangent, mlp_part
    )
    grad_input, layer_out, share, grad_qkv, grad_out = last(
        activations,
        label_rows,
        norm_gains,
        returned,
        packed,
        cosine,
        sine,
        gains_two,
        g_low,
        attn_sum,
        mlp_sum,
        g_mid,
        projections,
    )
    grad_gains, layer_out, grad_input, grad_qkv, grad_out, grad_up, grad_down = finish(
        norm_gains.shape[0] // 2,
        share,
        layer_out,
        grad_input,
        grad_qkv,
        grad_out,
        grad_up,
        down_low,
        down_high,
    )
    return (
        layer_out,
        grad_input,
        grad_gains,
        grad_qkv.transpose(1, 0, 2),
        grad_out,
        grad_up,
        grad_down,
    )


def solution(mesh):
    return jax.shard_map(
        per_device,
        mesh=mesh,
        in_specs=(
            P("tok", None),
            P("tok"),
            P("tok"),
            P(),
            P(None, None, "head"),
            P("head", None),
            P(None, "head"),
            P("head", None),
            P("tok", None),
        ),
        out_specs=(
            P("tok", None),
            P("tok", None),
            P(None, "tok"),
            P("tok", None, "head"),
            P(("head", "tok"), None),
            P("tok", "head"),
            P(("head", "tok"), None),
        ),
        check_vma=False,
    )
```

profile of v0, /device:TPU:0, one launch (start us, length us, event | category | flops | bytes accessed | tf_op | source)
XLA Modules:
  0.0 223.4 jit_solution(13253646286735105699)
XLA Ops:
  0.6 61.8 %attention_forward.1 = (bf16[4,256,128]{2,1,0:T(8,128)(2,1)}, bf16[4,2,4,272,256]{4,3,2,1,0:T(8,128)(2,1)}, f32[1024,128]{1,0:T(8,128)}, f32[8,1024]{1,0:T(8,128...) custom-call(bf16[256,2048]{1,0:T(8,128)(2,1)} %x_ref.5, ...), custom_call_target="tpu_custom_call" | custom-call | tf_op jit(solution)/shard_map/attention_forward/pallas_call | solution.py:729
  62.5 61.7 %middle.1 = (f32[256,2048]{1,0:T(8,128)}, bf16[256,2048]{1,0:T(8,128)(2,1)}, bf16[4,256,128]{2,1,0:T(8,128)(2,1)}, bf16[2,4,64,1024]{3,2,1,0:T(8,128)(2,1)}, bf1...) custom-call(bf16[256,2048]{1,0:T(8,128)(2,1)} %x_ref.5, ...), custom_call_target="tpu_custom_call" | custom-call | tf_op jit(solution)/shard_map/middle/pallas_call | solution.py:975
  124.2 50.3 %attention_backward.1 = (bf16[4,256,384]{2,1,0:T(8,128)(2,1)}, f32[64,1024]{1,0:T(8,128)}, bf16[2,4,64,1024]{3,2,1,0:T(8,128)(2,1)}) custom-call(bf16[4,256,128]{2,1,0:T(8,128)(2,1)} %get-tuple-element.46.grads, bf16[4,256,128]{2,1,0:T(8,128)(2,1)} %get-tuple-element.47.q_ref, bf16[4,2,4,272,256]{4,3,2,1,0:T(8,128)(2,1)} %get-tuple-element.48.kv_hbm, ...), custom_call_target="tpu_custom_call" | custom-call | tf_op jit(solution)/shard_map/attention_backward/pallas_call | solution.py:1213
  174.5 43.1 %last.1 = (f32[256,2048]{1,0:T(8,128)}, bf16[256,2048]{1,0:T(8,128)(2,1)}, f32[8,128]{1,0:T(8,128)}, f32[3,64,512]{2,1,0:T(8,128)}, f32[16,2048]{1,0:T(8,128)}) custom-call(bf16[256,2048]{1,0:T(8,128)(2,1)} %x_ref.5, s32[256,128]{1,0:T(8,128)} %get-tuple-element.42.labels_ref, f32[6,2048]{1,0:T(8,128)} %gains_ref.5, ...), custom_call_target="tpu_custom_call" | custom-call | tf_op jit(solution)/shard_map/last/pallas_call | solution.py:1417
  217.6 5.6 %finish.1 = (f32[6,64]{1,0:T(8,128)}, bf16[256,2048]{1,0:T(8,128)(2,1)}, f32[256,2048]{1,0:T(8,128)}, f32[3,64,512]{2,1,0:T(8,128)}, f32[16,2048]{1,0:T(8,128)}, /*index=5*/f32[64,2048]{1,0:T(8,128)}, f32[64,2048]{1,0:T(8,128)}) custom-call(f32[8,128]{1,0:T(8,128)} %get-tuple-element.62.share_ref, bf16[256,2048]{1,0:T(8,128)(2,1)} %get-tuple-element.63.layer_in, ...), custom_call_target="tpu_custom_call" | custom-call | tf_op jit(solution)/shard_map/finish/pallas_call | solution.py:1507
where the time goes:
time: 227 us; the launch traced here: 223 us
  Pallas kernels  222 us (98%)
    pallas_call x1, Pallas kernels, attention_forward(): pl.pallas_call(forward_kernel, out_shape=[jax.ShapeDtypeStruct((4, ROWS,...  61.8 us
    pallas_call x1, Pallas kernels, middle(): pl.pallas_call(middle_kernel, out_shape=[jax.ShapeDtypeStruct((ROWS, widt...  61.7 us
    pallas_call x1, Pallas kernels, attention_backward(): pl.pallas_call(backward_kernel, out_shape=[jax.ShapeDtypeStruct((4, ROWS,...  50.3 us
    pallas_call x1, Pallas kernels, last(): pl.pallas_call(last_kernel, out_shape=[jax.ShapeDtypeStruct((ROWS, width)...  43.1 us
    pallas_call x1, Pallas kernels, finish(): pl.pallas_call(finish_kernel, out_shape=[jax.ShapeDtypeStruct((2 * modes,...  5.56 us

commit v1 on v0

--- a/solution.py
+++ b/solution.py
@@ -79,44 +79,81 @@
             copy.wait_send()
 
 
+def advance(steps_left, count=1):
+    for _ in range(count):
+        next(steps_left)
+
+
+def ring_sum(copies, own, towards, source, block, slots):
+    up, down = towards(1), towards(-1)
+    from_down = copies.start(source(2, 0), slots.at[0], up, slots.at[0])
+    from_up = copies.start(source(2, 1), slots.at[1], down, slots.at[1])
+    raw_down = copies.start(source(1, 1), slots.at[2], up, slots.at[2])
+    raw_up = copies.start(source(-1, 0), slots.at[3], down, slots.at[3])
+    yield
+    from_down.wait_recv()
+    slots[0] = (block(1, 0)[...].astype(f32) + slots[0].astype(f32)).astype(bf16)
+    sum_down = copies.start(slots.at[0], slots.at[4], up, slots.at[4])
+    from_up.wait_recv()
+    slots[1] = (block(-1, 1)[...].astype(f32) + slots[1].astype(f32)).astype(bf16)
+    sum_up = copies.start(slots.at[1], slots.at[5], down, slots.at[5])
+    yield
+    for arrival in (raw_down, raw_up, sum_down, sum_up):
+        arrival.wait_recv()
+
+    def finished(half):
+        mine = block(0, half)[...].astype(f32)
+        if half == 0:
+            return mine + slots[4].astype(f32) + slots[3].astype(f32)
+        return mine + slots[2].astype(f32) + slots[5].astype(f32)
+
+    own.append(finished)
+
+
 def sum_over_y(copies, here, given, came, total):
     x, y, z, core = here
-    arrivals = []
-    for n, hop in enumerate(HOPS):
-        other = around(y, hop)
-        arrivals.append(
-            copies.start(given.at[other], came.at[n], device(x, other, z, core), came.at[n])
-        )
+    rows = given.shape[1] // 2
+    halves = (pl.ds(0, rows), pl.ds(rows, rows))
+
+    def towards(step):
+        return device(x, around(y, step), z, core)
+
+    def block(step, half):
+        return given.at[around(y, step), halves[half]]
+
+    done = []
+    ring = ring_sum(copies, done, towards, block, block, came)
+    next(ring)
     yield
-    for arrival in arrivals:
-        arrival.wait_recv()
-    total[y] = (
-        (given[y].astype(f32) + came[0].astype(f32))
-        + (came[1].astype(f32) + came[2].astype(f32))
-    ).astype(bf16)
-    arrivals = []
-    for hop in HOPS:
-        arrivals.append(
-            copies.start(
-                total.at[y],
-                total.at[y],
-                device(x, around(y, hop), z, core),
-                total.at[around(y, -hop)],
-            )
-        )
+    next(ring)
     yield
-    for arrival in arrivals:
-        arrival.wait_recv()
+    next(ring, None)
+    for half in range(2):
+        total[y, halves[half]] = done[0](half).astype(bf16)
+    last_y, next_y, far_y = around(y, -1), around(y, 1), around(y, 2)
+    mine = total.at[y]
+    from_last = copies.start(mine, mine, towards(1), total.at[last_y])
+    from_next = copies.start(mine, mine, towards(-1), total.at[next_y])
+    yield
+    from_last.wait_recv()
+    part = total.at[last_y, halves[0]]
+    far_low = copies.start(part, part, towards(1), total.at[far_y, halves[0]])
+    from_next.wait_recv()
+    part = total.at[next_y, halves[1]]
+    far_high = copies.start(part, part, towards(-1), total.at[far_y, halves[1]])
+    yield
+    far_low.wait_recv()
+    far_high.wait_recv()
     yield
 
 
 def sum_scratch(width):
     quarter = ROWS // SIDE
     return [
-        pltpu.VMEM((2, 3, quarter, width // 2), bf16),
+        pltpu.VMEM((2, 6, quarter // 2, width // 2), bf16),
         pltpu.VMEM((2, SIDE, quarter, width // 2), bf16),
-        pltpu.SemaphoreType.DMA((12,)),
-        pltpu.SemaphoreType.DMA((12,)),
+        pltpu.SemaphoreType.DMA((20,)),
+        pltpu.SemaphoreType.DMA((20,)),
     ]
 
 
@@ -127,53 +164,31 @@
     return jnp.concatenate(halves, axis=1).astype(f32)
 
 
-def ring_sum(copies, own, towards, block, slots):
-    up, down = towards(1), towards(-1)
-    from_down = copies.start(block(2, 0), slots.at[0], up, slots.at[0])
-    from_up = copies.start(block(2, 1), slots.at[1], down, slots.at[1])
-    raw_down = copies.start(block(1, 1), slots.at[2], up, slots.at[2])
-    raw_up = copies.start(block(-1, 0), slots.at[3], down, slots.at[3])
-    yield
-    from_down.wait_recv()
-    onward = block(1, 0)
-    onward[...] = (onward[...].astype(f32) + slots[0].astype(f32)).astype(bf16)
-    sum_down = copies.start(onward, slots.at[4], up, slots.at[4])
-    from_up.wait_recv()
-    onward = block(-1, 1)
-    onward[...] = (onward[...].astype(f32) + slots[1].astype(f32)).astype(bf16)
-    sum_up = copies.start(onward, slots.at[5], down, slots.at[5])
-    yield
-    for arrival in (raw_down, raw_up, sum_down, sum_up):
-        arrival.wait_recv()
-
-    def finished(half):
-        mine = block(0, half)[...].astype(f32)
-        if half == 0:
-            return mine + slots[4].astype(f32) + slots[3].astype(f32)
-        return mine + slots[2].astype(f32) + slots[5].astype(f32)
-
-    own.append(finished)
+WAYS = (0, 1, 0, 1)
+DOWN_WAYS = (0, 1, 0, 0)
 
 
 def ring_shapes(rows, cols):
     if rows >= 32:
         width = cols // 4
-        return 2, (2 * rows, width), (rows // 2, width)
-    return 1, (4 * rows, cols // 4), (rows, cols // 4)
+        return 4, (2 * rows, width), (rows // 2, width)
+    return 2, (4 * rows, cols // 4), (rows, cols // 4)
+
+
+def factor_scratch(rows, cols):
+    return [pltpu.VMEM((16, rows, 2 * ROWS), bf16), pltpu.VMEM((2 * ROWS, cols), bf16)]
 
 
 def weight_scratch(rows, cols):
-    chunks, first, late = ring_shapes(rows, cols)
+    groups, first, late = ring_shapes(rows, cols)
     return [
-        pltpu.VMEM((16, rows, 2 * ROWS), bf16),
-        pltpu.VMEM((2 * ROWS, cols), bf16),
-        pltpu.VMEM((2, chunks, 4, 2) + first, bf16),
-        pltpu.VMEM((2, chunks, 6) + first, bf16),
-        pltpu.VMEM((2, chunks, 4, 2) + late, bf16),
-        pltpu.VMEM((2, chunks, 6) + late, bf16),
-        pltpu.SemaphoreType.DMA((2 + 24 * chunks,)),
-        pltpu.SemaphoreType.DMA((2 + 24 * chunks,)),
-        pltpu.SemaphoreType.DMA((2,)),
+        pltpu.VMEM((groups, 4, 2) + first, bf16),
+        pltpu.VMEM((groups, 6) + first, bf16),
+        pltpu.VMEM((groups, 4, 2) + late, bf16),
+        pltpu.VMEM((groups, 6) + late, bf16),
+        pltpu.SemaphoreType.DMA((2 + 12 * groups,)),
+        pltpu.SemaphoreType.DMA((2 + 12 * groups,)),
+        pltpu.SemaphoreType.DMA((2 + 4 * groups,)),
     ]
 
 
@@ -198,64 +213,29 @@
     return dot(chosen, factor[:, 512 * group : 512 * (group + 1)], NT).astype(bf16)
 
 
-def weight_grad(here, left, right, out, scratch, far=None):
-    both_left, both_right, parts, came, sums, late, send_sems, recv_sems, own_sems = scratch
+def partial_block(both_left, both_right, way, at, group, width):
+    rows = both_left.shape[1]
+    if way == 0:
+        chosen = both_left[pl.ds(at * 4, 4)].reshape(4 * rows, 2 * ROWS)
+    else:
+        chosen = jnp.concatenate([both_left[k * 4 + at] for k in range(4)], axis=0)
+    return dot(chosen, both_right[:, group * width : (group + 1) * width]).astype(bf16)
+
+
+def weight_grad(here, out, scratch, factors=None, far=None, left=None, right=None, parts_hbm=None, ways=WAYS,
+                ready=None):
+    parts, came, sums, late, send_sems, recv_sems, own_sems = scratch
     x, y, z, core = here
-    rows, cols = both_left.shape[1], both_right.shape[1]
     copies = Copies(send_sems, recv_sems)
     twin = device(x, y, z, 1 - core)
-    if far is None:
-        far = left.at[:, 1 - core]
-        own_left = pltpu.make_async_copy(
-            left.at[:, core], both_left.at[:, :, pl.ds(0, ROWS)], own_sems.at[0]
-        )
-        own_right = pltpu.make_async_copy(right, both_right.at[pl.ds(0, ROWS)], own_sems.at[1])
-        own_left.start()
-        own_right.start()
-    else:
-        right = both_right.at[pl.ds(0, ROWS)]
-        own_left = own_right = None
-    far_left = copies.start(
-        far,
-        both_left.at[:, :, pl.ds(ROWS, ROWS)],
-        twin,
-        both_left.at[:, :, pl.ds(ROWS, ROWS)],
-    )
-    far_right = copies.start(
-        right,
-        both_right.at[pl.ds(ROWS, ROWS)],
-        twin,
-        both_right.at[pl.ds(ROWS, ROWS)],
-    )
-    yield
-    if own_left is not None:
-        own_left.wait()
-        own_right.wait()
-    far_left.wait_recv()
-    far_right.wait_recv()
-
-    chunks, first_shape, late_shape = ring_shapes(rows, cols)
-    by_rows = chunks == 2
-    width = cols // 2 // chunks
+    groups = parts.shape[0]
+    rows = out.shape[-2]
+    by_rows = groups == 4
+    first_shape, late_shape = parts.shape[3:], late.shape[2:]
+    width = first_shape[1] if by_rows else 2 * first_shape[1]
 
     def spot(way, step):
         return around(x if way == 0 else z, step)
-
-    def fill(way, chunk, step):
-        at = spot(way, step)
-        if way == 0:
-            chosen = both_left[pl.ds(at * 4, 4)].reshape(4 * rows, 2 * ROWS)
-        else:
-            chosen = jnp.concatenate([both_left[k * 4 + at] for k in range(4)], axis=0)
-        start = (way * chunks + chunk) * width
-        value = dot(chosen, both_right[:, start : start + width]).astype(bf16)
-        if by_rows:
-            parts[way, chunk, at] = value.reshape((2,) + first_shape)
-        else:
-            for half_index in range(2):
-                parts[way, chunk, at, half_index] = value[
-                    :, half_index * first_shape[1] : (half_index + 1) * first_shape[1]
-                ]
 
     def towards(way):
         def target(step):
@@ -265,69 +245,126 @@
 
         return target
 
-    every = [(way, chunk) for chunk in range(chunks) for way in (0, 1)]
-    first, first_done = {}, {}
-    for way, chunk in every:
-        for step in (2, 1, -1):
-            fill(way, chunk, step)
-        first_done[way, chunk] = []
-        first[way, chunk] = ring_sum(
+    waits = []
+    if parts_hbm is None:
+        both_left, both_right = factors
+    if parts_hbm is None and ready is None:
+        if left is not None:
+            far = left.at[:, 1 - core]
+            own = pltpu.make_async_copy(
+                left.at[:, core], both_left.at[:, :, pl.ds(0, ROWS)], own_sems.at[0]
+            )
+            own.start()
+            waits.append(own.wait)
+        if right is not None:
+            own = pltpu.make_async_copy(right, both_right.at[pl.ds(0, ROWS)], own_sems.at[1])
+            own.start()
+            waits.append(own.wait)
+        else:
+            right = both_right.at[pl.ds(0, ROWS)]
+        if far is not None:
+            theirs = both_left.at[:, :, pl.ds(ROWS, ROWS)]
+            waits.append(copies.start(far, theirs, twin, theirs).wait_recv)
+        theirs = both_right.at[pl.ds(ROWS, ROWS)]
+        waits.append(copies.start(right, theirs, twin, theirs).wait_recv)
+    elif ready is None:
+        for group in range(groups):
+            for n, (step, half_index) in enumerate(((1, 0), (-1, 1), (0, 0), (0, 1))):
+                at = spot(ways[group], step)
+                own = pltpu.make_async_copy(
+                    parts_hbm.at[group, at, half_index],
+                    parts.at[group, at, half_index],
+                    own_sems.at[2 + 4 * group + n],
+                )
+                own.start()
+                waits.append(own.wait)
+    yield
+
+    def fill(group, step):
+        at = spot(ways[group], step)
+        value = partial_block(both_left, both_right, ways[group], at, group, width)
+        if by_rows:
+            parts[group, at] = value.reshape((2,) + first_shape)
+        else:
+            for half_index in range(2):
+                parts[group, at, half_index] = value[
+                    :, half_index * first_shape[1] : (half_index + 1) * first_shape[1]
+                ]
+
+    if parts_hbm is None:
+        for wait in waits:
+            wait()
+        waits = []
+    source = parts if parts_hbm is None else parts_hbm
+    first, first_done, second, second_done = {}, {}, {}, {}
+    for group in range(4):
+        if group >= groups:
+            yield
+            continue
+        if ready is not None:
+            ready(group)
+        if parts_hbm is None:
+            for step in (2, 1, -1):
+                fill(group, step)
+        first_done[group] = []
+        first[group] = ring_sum(
             copies,
-            first_done[way, chunk],
-            towards(way),
-            lambda step, half_index, way=way, chunk=chunk: parts.at[
-                way, chunk, spot(way, step), half_index
-            ],
-            came.at[way, chunk],
-        )
-        next(first[way, chunk])
-    for way, chunk in every:
-        fill(way, chunk, 0)
+            first_done[group],
+            towards(ways[group]),
+            lambda step, half, group=group: source.at[group, spot(ways[group], step), half],
+            lambda step, half, group=group: parts.at[group, spot(ways[group], step), half],
+            came.at[group],
+        )
+        next(first[group])
+        yield
+    if parts_hbm is None:
+        for group in range(groups):
+            fill(group, 0)
+    for wait in waits:
+        wait()
     yield
-    for chunk in range(2):
-        for way in (0, 1):
-            if chunk < chunks:
-                next(first[way, chunk])
+    stages = [range(groups // 2), range(groups // 2, groups)] if by_rows else [range(groups), ()]
+    for stage in stages:
+        for group in stage:
+            next(first[group])
         yield
-    second, second_done = {}, {}
-    for chunk in range(2):
-        for way in (0, 1):
-            if chunk >= chunks:
-                continue
-            next(first[way, chunk], None)
-            finished = first_done[way, chunk][0]
+    for stage in stages:
+        for group in stage:
+            next(first[group], None)
             for half_index in (0, 1):
-                value = finished(half_index).astype(bf16)
+                value = first_done[group][0](half_index).astype(bf16)
                 if by_rows:
-                    sums[way, chunk, 2 * half_index : 2 * half_index + 2] = value.reshape(
+                    sums[group, 2 * half_index : 2 * half_index + 2] = value.reshape(
                         (2, 2) + late_shape
                     )
                 else:
-                    sums[way, chunk, :, half_index] = value.reshape((4,) + late_shape)
-            second_done[way, chunk] = []
-            second[way, chunk] = ring_sum(
+                    sums[group, :, half_index] = value.reshape((4,) + late_shape)
+            second_done[group] = []
+
+            def block(step, half, group=group):
+                return sums.at[group, spot(1 - ways[group], step), half]
+
+            second[group] = ring_sum(
                 copies,
-                second_done[way, chunk],
-                towards(1 - way),
-                lambda step, half_index, way=way, chunk=chunk: sums.at[
-                    way, chunk, spot(1 - way, step), half_index
-                ],
-                late.at[way, chunk],
+                second_done[group],
+                towards(1 - ways[group]),
+                block,
+                block,
+                late.at[group],
             )
-            next(second[way, chunk])
+            next(second[group])
         yield
-    for at in every:
-        next(second[at])
+    for group in range(groups):
+        next(second[group])
     yield
-    for way, chunk in every:
-        next(second[way, chunk], None)
-        start = (way * chunks + chunk) * width
+    for group in range(groups):
+        next(second[group], None)
         for half_index in (0, 1):
-            value = second_done[way, chunk][0](half_index)
+            value = second_done[group][0](half_index)
             if by_rows:
-                store_part(out, half_index * late_shape[0], start, value)
+                store_part(out, half_index * late_shape[0], group * width, value)
             else:
-                store_part(out, 0, start + half_index * late_shape[1], value)
+                store_part(out, 0, group * width + half_index * late_shape[1], value)
     copies.finish()
     yield
 
@@ -416,9 +453,9 @@
 
 def forward_kernel(
     x_ref, label_ref, position_ref, gains_ref, cotangent_ref, weight_hbm, out_weight_hbm, down_hbm,
-    q_all_ref, kv_all_ref, o_ref, lse_ref, returned_ref, total_ref, grad_active_hbm, weights_ref, tops_ref, labels_ref,
-    cos_ref, sin_ref,
-    grad_active_ref, weight, out_weight, down, weights, normed, q_own, kv_own, queries, keys_values, top, norm, acc, column, bounds_ref, o_low, back,
+    q_all_ref, kv_all_ref, o_ref, lse_ref, out_left_ref, total_ref, grad_active_hbm, weights_ref, tops_ref, labels_ref,
+    cos_ref, sin_ref, qkv_left_hbm, cotangent_both,
+    own_left, far_left, grad_active_ref, weight, out_weight, down, weights, normed, q_own, kv_own, queries, keys_values, top, norm, acc, column, bounds_ref, o_low, back,
     gathered, send_sems, recv_sems, load_sems, weight_sems,
 ):
     here = place()
@@ -435,7 +472,6 @@
     load = pltpu.make_async_copy(weight_hbm, weight, load_sems.at[1])
     load.start()
     load_down = pltpu.make_async_copy(down_hbm, down, load_sems.at[3])
-    load_down.start()
     copies = Copies(send_sems, recv_sems)
 
     position = position_ref[...]
@@ -499,6 +535,7 @@
         w_twin.append(copies.start(block, block, twin, out_weight.at[y_next, 1 - core, n]))
 
     load.wait()
+    load_down.start()
     cosine, sine = cos_ref[...], sin_ref[...]
 
     def rotate(values, head):
@@ -561,6 +598,27 @@
         at = slab(index, WIDE)
         grad_active_ref[:, at] = dot(cotangent_ref[...], down[at, :], NT)
 
+    keep_more = [
+        pltpu.make_async_copy(
+            cotangent_ref, cotangent_both.at[pl.ds(0, ROWS)], load_sems.at[5]
+        )
+    ]
+    theirs = cotangent_both.at[pl.ds(ROWS, ROWS)]
+    for_twin = [copies.start(cotangent_ref, theirs, twin, theirs)]
+    rows = far_left.shape[1]
+    for group in range(4):
+        at = pl.ds(4 * group, 4)
+        own_left[at] = pick(core, normed, rows, group).reshape(4, rows, ROWS)
+        far_left[at] = pick(1 - core, normed, rows, group).reshape(4, rows, ROWS)
+    keep_more.append(
+        pltpu.make_async_copy(
+            own_left, qkv_left_hbm.at[:, :, pl.ds(0, ROWS)], load_sems.at[6]
+        )
+    )
+    theirs = qkv_left_hbm.at[:, :, pl.ds(ROWS, ROWS)]
+    for_twin.append(copies.start(far_left, theirs, twin, theirs))
+    for copy in keep_more:
+        copy.start()
     half_steps = grad_active_ref.shape[1] // WIDE // 2
     keep_grad = pltpu.make_async_copy(grad_active_ref, grad_active_hbm, load_sems.at[4])
     steps(half_steps, grad_active)
@@ -688,32 +746,50 @@
         w_twin.append(copies.start(block, block, twin, out_weight.at[y_far, 1 - core, n]))
     take(came_back)
     local = 4 * HD
-    mine = pl.ds(pl.multiple_of(y * local, local), local)
     for n in range(4):
         gathered[y, :, n * HD : (n + 1) * HD] = back[n]
-    spread_y = [
-        copies.start(
-            gathered.at[y],
-            gathered.at[y],
-            device(x, around(y, hop), z, core),
-            gathered.at[around(y, -hop)],
-        )
-        for hop in HOPS
-    ]
-    returned_ref[...] = gathered[y]
+    half = ROWS // 2
+    block = gathered.at[y]
+    ring_last = copies.start(block, block, y_up, gathered.at[y_last])
+    ring_next = copies.start(block, block, y_down, gathered.at[y_next])
+    out_rows = out_left_ref.shape[2]
+    for core_at in range(2):
+        out_left_ref[:, core_at] = pick(core_at, gathered[y], out_rows, 0).reshape(
+            16, out_rows, ROWS
+        )
+    keep_grad.wait()
+    summed = grad_active_ref
+
+    def project(index, owners, first, final):
+        at = slab(index, WIDE)
+        part = sum(
+            dot(gathered[n], out_weight[n, :, :, :, at].reshape(local, WIDE)) for n in owners
+        )
+        if not first:
+            part = part + summed[:, at]
+        if final:
+            total_ref[:, at] = part.astype(bf16)
+        else:
+            summed[:, at] = part
+
+    count = total_ref.shape[1] // WIDE
+    steps(count, lambda index: project(index, (y,), True, False))
     take(w_twin)
-    take(spread_y)
-
-    def project(index):
-        at = slab(index, WIDE)
-        total_ref[:, at] = sum(
-            dot(gathered[n], out_weight[n, :, :, :, at].reshape(local, WIDE)) for n in range(4)
-        ).astype(bf16)
-
-    steps(total_ref.shape[1] // WIDE, project)
+    ring_last.wait_recv()
+    block = gathered.at[y_last, pl.ds(0, half)]
+    ring_low = copies.start(block, block, y_up, gathered.at[y_far, pl.ds(0, half)])
+    ring_next.wait_recv()
+    block = gathered.at[y_next, pl.ds(half, half)]
+    ring_high = copies.start(block, block, y_down, gathered.at[y_far, pl.ds(half, half)])
+    steps(count, lambda index: project(index, (y_last, y_next), False, False))
+    ring_low.wait_recv()
+    ring_high.wait_recv()
+    steps(count, lambda index: project(index, (y_far,), False, True))
     copies.finish()
     keep.wait()
-    keep_grad.wait()
+    for copy in keep_more:
+        copy.wait()
+    take(for_twin)
     for copy in stored[-2:]:
         copy.wait()
 
@@ -724,7 +800,8 @@
     width = out_weight.shape[1]
     whole = pl.BlockSpec(memory_space=pltpu.VMEM)
     anywhere = pl.BlockSpec(memory_space=pl.ANY)
-    count = 3 + 3 + 12 + 16 + 4 + 3 + 3 + 8 + 4 + 8 + 4
+    count = 3 + 3 + 12 + 16 + 4 + 3 + 4 + 8 + 4 + 8 + 4 + 2
+    local = out_weight.shape[0]
     pieces = (2, 4, out_weight.shape[0] // 8, width)
     return pl.pallas_call(
         forward_kernel,
@@ -733,7 +810,7 @@
             jax.ShapeDtypeStruct((4, 2, 4, ROWS + CODE_ROWS, 2 * HD), bf16),
             jax.ShapeDtypeStruct((4 * ROWS, HD), f32),
             jax.ShapeDtypeStruct((8, 4 * ROWS), f32),
-            jax.ShapeDtypeStruct((ROWS, 4 * HD), bf16),
+            jax.ShapeDtypeStruct((16, 2, local // 32, ROWS), bf16),
             jax.ShapeDtypeStruct((ROWS, width), bf16),
             jax.ShapeDtypeStruct((ROWS, down_weight.shape[0]), f32),
             jax.ShapeDtypeStruct((4, 2, 4 * ROWS, 4 * ROWS), bf16),
@@ -741,10 +818,18 @@
             jax.ShapeDtypeStruct((ROWS, HD), jnp.int32),
             jax.ShapeDtypeStruct((ROWS, HD), f32),
             jax.ShapeDtypeStruct((ROWS, HD), f32),
+            jax.ShapeDtypeStruct((16, width // 32, 2 * ROWS), bf16),
+            jax.ShapeDtypeStruct((2 * ROWS, width), bf16),
         ],
         in_specs=[whole] * 5 + [anywhere] * 3,
-        out_specs=[whole, anywhere] + [whole] * 4 + [anywhere, anywhere] + [whole] * 4,
+        out_specs=[whole, anywhere]
+        + [whole] * 4
+        + [anywhere, anywhere]
+        + [whole] * 4
+        + [anywhere] * 2,
         scratch_shapes=[
+            pltpu.VMEM((16, width // 32, ROWS), bf16),
+            pltpu.VMEM((16, width // 32, ROWS), bf16),
             pltpu.VMEM((ROWS, down_weight.shape[0]), f32),
             pltpu.VMEM(weight.shape, bf16),
             pltpu.VMEM((4,) + pieces, bf16),
@@ -765,7 +850,7 @@
             pltpu.VMEM((4, ROWS, 4 * HD), bf16),
             pltpu.SemaphoreType.DMA((count,)),
             pltpu.SemaphoreType.DMA((count,)),
-            pltpu.SemaphoreType.DMA((5,)),
+            pltpu.SemaphoreType.DMA((7,)),
             pltpu.SemaphoreType.DMA((2,)),
         ],
         compiler_params=pltpu.CompilerParams(
@@ -795,9 +880,10 @@
 
 def middle_kernel(
     x_ref, attn_ref, labels_ref, gains_ref, cotangent_hbm, out_weight_hbm, grad_active_hbm, up_hbm, down_hbm,
-    g_mid_hbm, g_low_hbm, heads_ref, mlp_hbm, active_left_hbm, gains_out_ref, grad_up_ref, grad_down_ref,
-    up, down, cotangent, out_weight, grad_active, g_mid, g_low, mlp, active_left, xhat, inverse, normed, active,
-    far, far_down, given, g_heads, came, all_rows, y_send, y_recv, load_sems, x_send, x_recv, *more,
+    g_mid_hbm, g_low_hbm, heads_ref, mlp_hbm, down_parts_hbm, gains_out_ref, grad_up_ref,
+    up, down, out_weight, grad_active, g_mid, g_low, mlp, xhat, inverse, normed, active, far, far_down, down_left,
+    down_right, down_parts, given, g_heads, came, all_rows, y_send, y_recv, load_sems, x_send, x_recv,
+    exchange_send, exchange_recv, both_left, both_right, *up_scratch,
 ):
     here = place()
     x, y, z, core = here
@@ -807,9 +893,6 @@
         + [device(x, y, around(z, hop), core) for hop in (1, 3)]
         + [device(x, y, z, 1 - core)]
     )
-    up_scratch, down_scratch = more[:9], more[9:]
-    both_left, both_right = up_scratch[:2]
-    down_left, down_right = down_scratch[:2]
     used = [0]
 
     def move(src, dst):
@@ -820,12 +903,6 @@
 
     load_up = move(up_hbm, up)
     load_active = move(grad_active_hbm, grad_active)
-    load_part = move(
-        cotangent_hbm.at[:, pl.ds(0, down_right.shape[1])], down_right.at[pl.ds(0, ROWS)]
-    )
-    load_down = move(down_hbm, down)
-    load_cotangent = move(cotangent_hbm, cotangent)
-    load_out = move(out_weight_hbm, out_weight)
     width = x_ref.shape[1]
     hidden_width = up.shape[1]
 
@@ -847,48 +924,46 @@
         far[at] = pick(1 - core, normed, rows, group).reshape(4, rows, ROWS)
     load_up.wait()
     load_active.wait()
-
-    def feed(index):
-        at = slab(index, WIDE)
+    load_down = move(down_hbm, down)
+    load_cotangent = move(cotangent_hbm, down_right)
+    load_out = move(out_weight_hbm, out_weight)
+    arrived()
+    twin = device(x, y, z, 1 - core)
+    exchange = Copies(exchange_send, exchange_recv)
+    theirs = both_left.at[:, :, pl.ds(ROWS, ROWS)]
+    left_came = exchange.start(far, theirs, twin, theirs)
+    right_came = []
+    for index in range(hidden_width // WIDE):
+        at = pl.ds(index * WIDE, WIDE)
         hidden = dot(normed[...], up[:, at])
         value, slope = gelu_and_slope(hidden)
         active[:, at] = value.astype(bf16)
         both_right[pl.ds(0, ROWS), at] = (grad_active[:, at] * slope).astype(bf16)
-
-    steps(hidden_width // WIDE, feed)
-    arrived()
-    ring = weight_grad(here, None, None, grad_up_ref, up_scratch, far)
-    next(ring)
-
+        theirs = both_right.at[pl.ds(ROWS, ROWS), at]
+        right_came.append(
+            exchange.start(both_right.at[pl.ds(0, ROWS), at], theirs, twin, theirs)
+        )
+
+    def ready(group):
+        if group == 0:
+            left_came.wait_recv()
+        right_came[group].wait_recv()
+
+    ring = weight_grad(here, grad_up_ref, up_scratch, (both_left, both_right), ready=ready)
+    advance(ring)
     copies = Copies(y_send, y_recv)
     half_steps = width // WIDE // 2
-    over_y = []
-    for half in range(2):
-
-        def back_up(index, half=half):
-            at = slab(index + half * half_steps, WIDE)
-            part = dot(both_right[pl.ds(0, ROWS), :], up[at, :], NT)
-            given[half, :, :, slab(index, WIDE)] = part.astype(bf16).reshape(
-                SIDE, ROWS // SIDE, WIDE
-            )
-
-        steps(half_steps, back_up)
-        over_y.append(
-            sum_over_y(copies, here, given.at[half], came.at[half], all_rows.at[half])
-        )
-        next(over_y[half])
-    next(ring)
-    for group in range(4):
-        at = pl.ds(4 * group, 4)
-        for core_at in range(2):
-            active_left[at, core_at] = pick(core_at, active, rows, group).reshape(4, rows, ROWS)
-        down_left[at, :, pl.ds(0, ROWS)] = active_left[at, core]
-        far_down[at] = active_left[at, 1 - core]
-    load_part.wait()
-    keep = [move(active_left, active_left_hbm)]
-    ring_down = weight_grad(here, None, None, grad_down_ref, down_scratch, far_down)
-    next(ring_down)
-    load_down.wait()
+    over_y = [
+        sum_over_y(copies, here, given.at[half], came.at[half], all_rows.at[half])
+        for half in range(2)
+    ]
+
+    def back_up(index, half):
+        at = slab(index + half * half_steps, WIDE)
+        part = dot(both_right[pl.ds(0, ROWS), :], up[at, :], NT)
+        given[half, :, :, slab(index, WIDE)] = part.astype(bf16).reshape(
+            SIDE, ROWS // SIDE, WIDE
+        )
 
     def feed_out(index, half):
         at = slab(index + half * half_steps, WIDE)
@@ -896,21 +971,52 @@
             dot(active[...], down[:, at]).astype(bf16).reshape(SIDE, ROWS // SIDE, WIDE)
         )
 
-    steps(half_steps, lambda index: feed_out(index, 0))
-    next(over_y[0])
-    next(ring_down)
-    steps(half_steps, lambda index: feed_out(index, 1))
+    groups, first_shape = down_parts.shape[0], down_parts.shape[3:]
+    keep = []
+
+    def fill_down(group):
+        for at in range(4):
+            down_parts[group, at] = partial_block(
+                down_left, down_right, DOWN_WAYS[group], at, group, first_shape[1]
+            ).reshape((2,) + first_shape)
+        keep.append(move(down_parts.at[group], down_parts_hbm.at[group]))
+
+    steps(half_steps, lambda index: back_up(index, 0))
+    advance(over_y[0])
+    advance(ring)
+    steps(half_steps, lambda index: back_up(index, 1))
+    advance(over_y[1])
+    advance(ring, 2)
+    advance(over_y[0])
+    advance(ring, 2)
+    load_down.wait()
+    feed_out(0, 0)
+    advance(over_y[1])
+    feed_out(1, 0)
+    advance(over_y[0])
+    feed_out(0, 1)
+    advance(over_y[1])
+    feed_out(1, 1)
     keep.append(move(mlp, mlp_hbm))
-    next(over_y[1])
-    next(ring)
-    next(ring)
+    for group in range(4):
+        at = pl.ds(4 * group, 4)
+        down_left[at, :, pl.ds(0, ROWS)] = pick(core, active, rows, group).reshape(4, rows, ROWS)
+        far_down[at] = pick(1 - core, active, rows, group).reshape(4, rows, ROWS)
+    theirs = down_left.at[:, :, pl.ds(ROWS, ROWS)]
+    down_came = exchange.start(far_down, theirs, twin, theirs)
+    advance(over_y[0])
+    advance(ring)
+    advance(over_y[1])
     load_cotangent.wait()
+    down_came.wait_recv()
+    fill_down(0)
+    advance(ring)
+    fill_down(1)
+    advance(ring)
     load_out.wait()
     gains_out_ref[...] = jnp.zeros_like(gains_out_ref)
-    next(over_y[0])
-    next(ring_down)
-    next(ring)
-    next(over_y[1])
+    advance(over_y[0])
+    advance(over_y[1])
 
     def back(index):
         at = slab(index, NORM_ROWS)
@@ -926,7 +1032,7 @@
         grad = grad * gain
         mean = jnp.mean(grad, axis=-1, keepdims=True)
         along = jnp.mean(product * gain, axis=-1, keepdims=True)
-        total = cotangent[at, :].astype(f32) + inverse[at, :1] * (grad - mean - unit * along)
+        total = down_right[at, :].astype(f32) + inverse[at, :1] * (grad - mean - unit * along)
         g_mid[at, :] = total
         g_low[at, :] = total.astype(bf16)
 
@@ -946,18 +1052,16 @@
     ]
     heads_ref[x] = g_heads[x]
     keep += [move(g_mid, g_mid_hbm), move(g_low, g_low_hbm)]
-    next(ring_down)
-    next(ring)
-    next(ring_down)
-    next(ring)
-    next(ring_down)
+    advance(ring)
+    fill_down(2)
+    advance(ring)
+    fill_down(3)
+    advance(ring)
     for arrival in arrivals:
         arrival.wait_recv()
-    next(ring)
-    next(ring_down)
-    next(ring_down)
     copies.finish()
     x_copies.finish()
+    exchange.finish()
     for copy in keep:
         copy.wait()
 
@@ -971,7 +1075,8 @@
     whole = pl.BlockSpec(memory_space=pltpu.VMEM)
     anywhere = pl.BlockSpec(memory_space=pl.ANY)
     summed = (2, SIDE, ROWS // SIDE, width // 2)
-    left = (16, 2, down_rows, ROWS)
+    groups, first_shape, late_shape = ring_shapes(down_rows, width)
+    down_parts = (groups, 4, 2) + first_shape
     return pl.pallas_call(
         middle_kernel,
         out_shape=[
@@ -979,37 +1084,39 @@
             jax.ShapeDtypeStruct((ROWS, width), bf16),
             jax.ShapeDtypeStruct((4, ROWS, HD), bf16),
             jax.ShapeDtypeStruct(summed, bf16),
-            jax.ShapeDtypeStruct(left, bf16),
+            jax.ShapeDtypeStruct(down_parts, bf16),
             jax.ShapeDtypeStruct((8, width), f32),
             jax.ShapeDtypeStruct((rows, hidden_width), f32),
-            jax.ShapeDtypeStruct((down_rows, width // 2), f32),
         ],
         in_specs=[whole] * 4 + [anywhere] * 5,
-        out_specs=[anywhere] * 2 + [whole] + [anywhere] * 2 + [whole] * 3,
+        out_specs=[anywhere] * 2 + [whole] + [anywhere] * 2 + [whole] * 2,
         scratch_shapes=[
             pltpu.VMEM(up_weight.shape, bf16),
             pltpu.VMEM(down_weight.shape, bf16),
-            pltpu.VMEM((ROWS, width), bf16),
             pltpu.VMEM(out_weight.shape, bf16),
             pltpu.VMEM((ROWS, hidden_width), f32),
             pltpu.VMEM((ROWS, width), f32),
             pltpu.VMEM((ROWS, width), bf16),
             pltpu.VMEM(summed, bf16),
-            pltpu.VMEM(left, bf16),
             pltpu.VMEM((ROWS, width), f32),
             pltpu.VMEM((ROWS, HD), f32),
             pltpu.VMEM((ROWS, width), bf16),
             pltpu.VMEM((ROWS, hidden_width), bf16),
             pltpu.VMEM((16, rows, ROWS), bf16),
             pltpu.VMEM((16, down_rows, ROWS), bf16),
+        ]
+        + factor_scratch(down_rows, width)
+        + [
+            pltpu.VMEM(down_parts, bf16),
             pltpu.VMEM(summed, bf16),
             pltpu.VMEM((4, ROWS, HD), bf16),
         ]
         + sum_scratch(width)
-        + [pltpu.SemaphoreType.DMA((10,))]
+        + [pltpu.SemaphoreType.DMA((12,))]
         + [pltpu.SemaphoreType.DMA((3,)), pltpu.SemaphoreType.DMA((3,))]
-        + weight_scratch(rows, hidden_width)
-        + weight_scratch(down_rows, width // 2),
+        + [pltpu.SemaphoreType.DMA((6,)), pltpu.SemaphoreType.DMA((6,))]
+        + factor_scratch(rows, hidden_width)
+        + weight_scratch(rows, hidden_width),
         compiler_params=pltpu.CompilerParams(
             collective_id=2, has_side_effects=True, vmem_limit_bytes=VMEM_LIMIT
         ),
@@ -1028,10 +1135,10 @@
 
 
 def backward_kernel(
-    grads, q_ref, kv_hbm, o_ref, lse_ref, tops_ref, weights_hbm, left_ref, right_ref, given_ref,
-    packed_ref, weight_ref, total_ref,
+    grads, q_ref, kv_hbm, o_ref, lse_ref, tops_ref, weights_hbm, down_parts_hbm, out_left_hbm, g_low_hbm, given_ref,
+    packed_ref, grad_down_ref, grad_out_ref, total_ref,
     keys_values, weights, delta, grad_q, parts, met, came, sums, q_low, back_q,
-    back_kv, send_sems, recv_sems, load_sems, weight_sems, y_came, all_rows, y_send, y_recv, *weight_scratch_refs,
+    back_kv, send_sems, recv_sems, load_sems, weight_sems, y_came, all_rows, y_send, y_recv, *more,
 ):
     here = place()
     x, y, z, core = here
@@ -1067,20 +1174,21 @@
         sum_over_y(y_copies, here, given_ref.at[half], y_came.at[half], all_rows.at[half])
         for half in range(2)
     ]
-    half = weight_ref.shape[1]
-    ring = weight_grad(
-        here, left_ref, right_ref.at[:, pl.ds(half, half)], weight_ref, weight_scratch_refs
-    )
+    ring = weight_grad(here, grad_down_ref, more[:7], parts_hbm=down_parts_hbm, ways=DOWN_WAYS)
+    ring_out = weight_grad(
+        here, grad_out_ref, more[9:], more[7:9], left=out_left_hbm, right=g_low_hbm
+    )
+    arrived()
+    advance(ring, 5)
+    for half in over_y:
+        advance(half)
+    advance(ring_out)
     grad_q[...] = jnp.zeros_like(grad_q)
     product = grads[...].reshape(4 * ROWS, HD).astype(f32) * o_ref[...]
     delta[...] = lax.dot_general(
         jnp.ones((8, HD), f32), product, NT, preferred_element_type=f32, precision=highest
     )
     load.wait()
-    arrived()
-    next(ring)
-    for half in over_y:
-        next(half)
     done = []
 
     def chunk(z_at, core_at):
@@ -1121,7 +1229,7 @@
     above, below = device(x, y, next_z, core), device(x, y, last_z, core)
     chunk(far_z, 1 - core)
     far_met = hand_over(far_z)
-    next(ring)
+    advance(ring_out, 5)
     chunk(far_z, core)
     chunk(next_z, 1 - core)
     next_met = hand_over(next_z)
@@ -1129,16 +1237,17 @@
     join(far_z)
     from_last = copies.start(parts.at[far_z, core, 0], came.at[0], above, came.at[0])
     from_next = copies.start(parts.at[far_z, core, 1], came.at[1], below, came.at[1])
+    for half in over_y:
+        advance(half)
+    advance(ring, 2)
     chunk(next_z, core)
-    next(ring)
     chunk(last_z, 1 - core)
     last_met = hand_over(last_z)
     next_met.wait_recv()
     join(next_z)
     raw_last = copies.start(parts.at[next_z, core, 1], came.at[2], above, came.at[2])
     for half in over_y:
-        next(half)
-    next(ring)
+        advance(half)
     chunk(last_z, core)
     chunk(z, 1 - core)
     own_met = hand_over(z)
@@ -1155,6 +1264,10 @@
         parts[last_z, core, 1].astype(f32) + came[1].astype(f32)
     ).astype(bf16)
     sum_next = copies.start(parts.at[last_z, core, 1], came.at[5], below, came.at[5])
+    for half in over_y:
+        advance(half)
+    advance(ring)
+    advance(ring_out)
     chunk(z, core)
     q_low[...] = (grad_q[...] * (HD**-0.5)).T.astype(bf16).reshape(4, ROWS, HD)
     arrivals = []
@@ -1169,7 +1282,8 @@
             )
         )
     back_q[x] = q_low[x]
-    next(ring)
+    advance(ring)
+    advance(ring_out, 2)
     own_met.wait_recv()
     raw_last.wait_recv()
     raw_next.wait_recv()
@@ -1192,11 +1306,13 @@
         )
     back_kv[x] = sums[x]
     for half in over_y:
-        next(half)
+        advance(half)
     total_ref[...] = all_rows[...]
-    next(ring)
-    next(ring)
-    next(ring)
+    advance(ring)
+    advance(ring_out, 2)
+    advance(ring)
+    advance(ring_out)
+    advance(ring)
     for arrival in arrivals:
         arrival.wait_recv()
     for n in range(4):
@@ -1206,19 +1322,24 @@
     y_copies.finish()
 
 
-def attention_backward(grad_heads, q_all, kv_all, o_all, lse, tops, weights, left, right, given):
+def attention_backward(
+    grad_heads, q_all, kv_all, o_all, lse, tops, weights, down_parts, out_left, g_low, given
+):
     whole = pl.BlockSpec(memory_space=pltpu.VMEM)
     anywhere = pl.BlockSpec(memory_space=pl.ANY)
     count = 4 + 6 + 6
+    width = g_low.shape[1]
+    down_rows, out_rows = down_parts.shape[3] // 2, out_left.shape[2]
     return pl.pallas_call(
         backward_kernel,
         out_shape=[
             jax.ShapeDtypeStruct((4, ROWS, 3 * HD), bf16),
-            jax.ShapeDtypeStruct((left.shape[2], right.shape[1] // 2), f32),
+            jax.ShapeDtypeStruct((down_rows, width), f32),
+            jax.ShapeDtypeStruct((out_rows, width), f32),
             jax.ShapeDtypeStruct(given.shape, bf16),
         ],
-        in_specs=[whole, whole, anywhere] + [whole] * 3 + [anywhere] * 3 + [whole],
-        out_specs=[whole, whole, whole],
+        in_specs=[whole, whole, anywhere] + [whole] * 3 + [anywhere] * 4 + [whole],
+        out_specs=[whole] * 4,
         scratch_shapes=[
             pltpu.VMEM((4, 2, 4, ROWS + CODE_ROWS, 2 * HD), bf16),
             pltpu.VMEM((3, 4 * ROWS, 4 * ROWS), bf16),
@@ -1237,40 +1358,42 @@
             pltpu.SemaphoreType.DMA((3,)),
         ]
         + sum_scratch(2 * given.shape[3])
-        + weight_scratch(left.shape[2], right.shape[1] // 2),
+        + weight_scratch(down_rows, width)
+        + factor_scratch(out_rows, width)
+        + weight_scratch(out_rows, width),
         compiler_params=pltpu.CompilerParams(
             collective_id=1, has_side_effects=True, vmem_limit_bytes=VMEM_LIMIT
         ),
         name="attention_backward",
-    )(grad_heads, q_all, kv_all, o_all, lse, tops, weights, left, right, given)
+    )(
+        grad_heads, q_all, kv_all, o_all, lse, tops, weights, down_parts, out_left, g_low, given
+    )
 
 
 def last_kernel(
-    x_ref, labels_ref, gains_ref, returned_ref, packed_ref, cos_ref, sin_ref, gains_two_ref, g_low_hbm, attn_hbm,
-    mlp_hbm, g_mid_hbm, weight_hbm,
-    input_ref, layer_ref, gains_out_ref, grad_qkv_ref, grad_out_ref,
-    attn, mlp, g_mid, weight, xhat, inverse, normed, far_qkv, far_out, given, gains_part, gains_given, came, all_rows, y_send, y_recv,
-    load_sems, *more,
+    x_ref, labels_ref, gains_ref, packed_ref, cos_ref, sin_ref, gains_two_ref, left_hbm, attn_hbm, mlp_hbm, g_mid_hbm,
+    weight_hbm,
+    input_ref, layer_ref, gains_out_ref, grad_qkv_ref,
+    attn, mlp, g_mid, weight, xhat, inverse, given, gains_part, gains_given, came, all_rows, y_send, y_recv, load_sems,
+    qkv_left, qkv_right, *more,
 ):
     gain_scratch = more[: len(GAIN_SCRATCH)]
     gain_send, gain_recv = more[len(GAIN_SCRATCH) : len(GAIN_SCRATCH) + 2]
-    qkv_scratch = more[len(GAIN_SCRATCH) + 2 : len(GAIN_SCRATCH) + 11]
-    out_scratch = more[len(GAIN_SCRATCH) + 11 :]
+    qkv_scratch = more[len(GAIN_SCRATCH) + 2 :]
     here = place()
     x, y, z, core = here
-    out_left, out_right = out_scratch[:2]
     loads = []
     for n, (src, dst) in enumerate(
         (
             (weight_hbm, weight),
-            (g_low_hbm, out_right.at[pl.ds(0, ROWS)]),
+            (left_hbm, qkv_left),
             (attn_hbm, attn),
             (mlp_hbm, mlp),
             (g_mid_hbm, g_mid),
         )
     ):
         loads.append(pltpu.make_async_copy(src, dst, load_sems.at[n]))
-        loads[n].start()
+    loads[0].start()
     arrived = greet(
         [device(x, around(y, hop), z, core) for hop in HOPS]
         + [device(around(x, hop), y, z, core) for hop in HOPS]
@@ -1278,9 +1401,7 @@
         + [device(x, y, z, 1 - core)]
     )
     width = x_ref.shape[1]
-    local = returned_ref.shape[1]
-    qkv_left, qkv_right = qkv_scratch[:2]
-    qkv_rows, out_rows = grad_qkv_ref.shape[1], grad_out_ref.shape[0]
+    local = qkv_right.shape[1] // 3
 
     cosine, sine = cos_ref[...], sin_ref[...]
     for head in range(4):
@@ -1295,6 +1416,39 @@
                 ).astype(bf16)
             start = part * local + head * HD
             qkv_right[0:ROWS, start : start + HD] = grad
+    arrived()
+    ring = weight_grad(here, grad_qkv_ref, qkv_scratch, (qkv_left, qkv_right))
+    advance(ring)
+    loads[0].wait()
+    for load in loads[1:]:
+        load.start()
+    copies = Copies(y_send, y_recv)
+    half_steps = width // WIDE // 2
+    over_y = [
+        sum_over_y(copies, here, given.at[half], came.at[half], all_rows.at[half])
+        for half in range(2)
+    ]
+
+    def back_in(index, half):
+        at = slab(index + half * half_steps, WIDE)
+        part = sum(
+            dot(qkv_right[pl.ds(0, ROWS), k * local : (k + 1) * local], weight[k, at, :], NT)
+            for k in range(3)
+        )
+        given[half, :, :, slab(index, WIDE)] = part.astype(bf16).reshape(
+            SIDE, ROWS // SIDE, WIDE
+        )
+
+    steps(half_steps, lambda index: back_in(index, 0))
+    advance(over_y[0])
+    loads[1].wait()
+    advance(ring)
+    steps(half_steps, lambda index: back_in(index, 1))
+    advance(over_y[1])
+    advance(ring, 2)
+    advance(over_y[0])
+    advance(ring, 2)
+    gains_part[...] = 0.25 * gains_two_ref[...]
 
     def norm(index):
         at = slab(index, NORM_ROWS)
@@ -1304,55 +1458,19 @@
         unit = centred * scale
         xhat[at, :] = unit
         inverse[at, :] = jnp.broadcast_to(scale, (NORM_ROWS, HD))
-        normed[at, :] = (unit * gain_rows(labels_ref[at, :1], gains_ref, 0)).astype(bf16)
-
-    steps(ROWS // NORM_ROWS, norm)
-    for group in range(4):
-        at = pl.ds(4 * group, 4)
-        qkv_left[at, :, pl.ds(0, ROWS)] = pick(core, normed, qkv_rows, group).reshape(
-            4, qkv_rows, ROWS
-        )
-        far_qkv[at] = pick(1 - core, normed, qkv_rows, group).reshape(4, qkv_rows, ROWS)
-    out_left[:, :, pl.ds(0, ROWS)] = pick(core, returned_ref, out_rows, 0).reshape(
-        16, out_rows, ROWS
-    )
-    far_out[...] = pick(1 - core, returned_ref, out_rows, 0).reshape(16, out_rows, ROWS)
-    arrived()
-    rings = [
-        weight_grad(here, None, None, grad_qkv_ref, qkv_scratch, far_qkv),
-        weight_grad(here, None, None, grad_out_ref, out_scratch, far_out),
-    ]
-    loads[1].wait()
-    for ring in rings:
-        next(ring)
-    loads[0].wait()
-    gains_part[...] = 0.25 * gains_two_ref[...]
-    copies = Copies(y_send, y_recv)
-    half_steps = width // WIDE // 2
-    over_y = []
-    for half in range(2):
-
-        def back_in(index, half=half):
-            at = slab(index + half * half_steps, WIDE)
-            part = sum(
-                dot(qkv_right[pl.ds(0, ROWS), k * local : (k + 1) * local], weight[k, at, :], NT)
-                for k in range(3)
+        labels = labels_ref[at, :1]
+        product = summed_rows(given, index) * unit
+        for mode in range(3):
+            gains_part[mode : mode + 1, :] += jnp.sum(
+                jnp.where(labels == mode, product, 0.0), axis=0, keepdims=True
             )
-            given[half, :, :, slab(index, WIDE)] = part.astype(bf16).reshape(
-                SIDE, ROWS // SIDE, WIDE
-            )
-            product = part * xhat[:, at]
-            labels = labels_ref[:, :1]
-            for mode in range(3):
-                gains_part[mode : mode + 1, at] = jnp.sum(
-                    jnp.where(labels == mode, product, 0.0), axis=0, keepdims=True
-                )
-
-        steps(half_steps, back_in)
-        over_y.append(
-            sum_over_y(copies, here, given.at[half], came.at[half], all_rows.at[half])
-        )
-        next(over_y[half])
+
+    norm_steps = ROWS // NORM_ROWS // 2
+    steps(norm_steps, norm)
+    advance(over_y[1])
+    advance(over_y[0])
+    steps(norm_steps, lambda index: norm(index + norm_steps))
+    advance(over_y[1])
     for owner in range(32):
         gains_given[owner // 8, (owner // 2) % 4, owner % 2] = jnp.zeros((8, HD), f32)
         gains_given[owner // 8, (owner // 2) % 4, owner % 2, :, :64] = gains_part[
@@ -1360,9 +1478,8 @@
         ]
     gain_copies = Copies(gain_send, gain_recv)
     over_all = sum_gains(gain_copies, here, gains_given, *gain_scratch, gains_out_ref)
-    next(over_all)
-    for ring in rings:
-        next(ring)
+    advance(over_all)
+    advance(ring)
     for load in loads[2:]:
         load.wait()
 
@@ -1372,19 +1489,14 @@
         layer_ref[at, :] = total.astype(bf16)
 
     steps(ROWS // NORM_ROWS, finish_layer)
-    next(over_y[0])
-    for ring in rings:
-        next(ring)
-    next(over_all)
-    next(over_y[1])
-    for step in range(2):
-        for ring in rings:
-            next(ring)
-    next(over_y[0])
-    for ring in rings:
-        next(ring)
-    next(over_all)
-    next(over_y[1])
+    advance(over_y[0])
+    advance(over_all)
+    advance(ring)
+    advance(over_y[1])
+    advance(over_y[0])
+    advance(ring)
+    advance(over_all)
+    advance(over_y[1])
 
     def finish_input(index):
         at = slab(index, NORM_ROWS)
@@ -1395,21 +1507,20 @@
         input_ref[at, :] = g_mid[at, :] + inverse[at, :1] * (grad - mean - unit * along)
 
     steps(ROWS // NORM_ROWS, finish_input)
-    for ring in rings:
-        next(ring)
-    next(over_all)
-    for ring in rings:
-        next(ring)
-    next(over_all)
+    advance(ring)
+    advance(over_all)
+    advance(ring)
+    advance(over_all)
+    advance(ring)
     copies.finish()
     gain_copies.finish()
 
 
 def last(
-    activations, labels, gains, returned, packed, cosine, sine, gains_two, g_low, attn_sum, mlp_sum, g_mid, weight
+    activations, labels, gains, packed, cosine, sine, gains_two, left, attn_sum, mlp_sum, g_mid, weight
 ):
     width = activations.shape[1]
-    local = returned.shape[1]
+    local = weight.shape[2]
     cols = 3 * local
     rows = width // 32
     whole = pl.BlockSpec(memory_space=pltpu.VMEM)
@@ -1421,10 +1532,9 @@
             jax.ShapeDtypeStruct((ROWS, width), bf16),
             jax.ShapeDtypeStruct((8, HD), f32),
             jax.ShapeDtypeStruct((3, rows, local), f32),
-            jax.ShapeDtypeStruct((local // 32, width), f32),
         ],
-        in_specs=[whole] * 8 + [anywhere] * 5,
-        out_specs=[whole] * 5,
+        in_specs=[whole] * 7 + [anywhere] * 5,
+        out_specs=[whole] * 4,
         scratch_shapes=[
             pltpu.VMEM(attn_sum.shape, bf16),
             pltpu.VMEM(mlp_sum.shape, bf16),
@@ -1432,19 +1542,16 @@
             pltpu.VMEM(weight.shape, bf16),
             pltpu.VMEM((ROWS, width), f32),
             pltpu.VMEM((ROWS, HD), f32),
-            pltpu.VMEM((ROWS, width), bf16),
-            pltpu.VMEM((16, rows, ROWS), bf16),
-            pltpu.VMEM((16, local // 32, ROWS), bf16),
             pltpu.VMEM(mlp_sum.shape, bf16),
             pltpu.VMEM((8, width), f32),
             pltpu.VMEM((4, 4, 2, 8, HD), f32),
         ]
         + sum_scratch(width)
         + [pltpu.SemaphoreType.DMA((5,))]
+        + factor_scratch(rows, cols)
         + [pltpu.VMEM(shape, f32) for shape in GAIN_SCRATCH]
         + [pltpu.SemaphoreType.DMA((10,)), pltpu.SemaphoreType.DMA((10,))]
-        + weight_scratch(rows, cols)
-        + weight_scratch(local // 32, width),
+        + weight_scratch(rows, cols),
         compiler_params=pltpu.CompilerParams(
             collective_id=3, has_side_effects=True, vmem_limit_bytes=VMEM_LIMIT
         ),
@@ -1453,12 +1560,11 @@
         activations,
         labels,
         gains,
-        returned,
         packed,
         cosine,
         sine,
         gains_two,
-        g_low,
+        left,
         attn_sum,
         mlp_sum,
         g_mid,
@@ -1467,17 +1573,15 @@
 
 
 def finish_kernel(
-    share_ref, layer_in, input_in, qkv_in, out_in, up_in, low_in, high_in,
+    share_ref, layer_in, input_in, qkv_in, out_in, up_in, down_in,
     gains_ref, layer_out, input_out, qkv_out, out_out, up_out, down_out,
-    layer, grad_input, qkv, out, up, low, high, load_sems, store_sems,
+    layer, grad_input, qkv, out, up, down, load_sems, store_sems,
 ):
-    half = low_in.shape[1]
     ways = (
         (layer_in, layer, layer_out),
         (up_in, up, up_out),
         (qkv_in, qkv, qkv_out),
-        (low_in, low, down_out.at[:, pl.ds(0, half)]),
-        (high_in, high, down_out.at[:, pl.ds(half, half)]),
+        (down_in, down, down_out),
         (out_in, out, out_out),
         (input_in, grad_input, input_out),
     )
@@ -1497,25 +1601,20 @@
         store.wait()
 
 
-def finish(modes, share, layer, grad_input, qkv, out, up, low, high):
+def finish(modes, share, *arrays):
     whole = pl.BlockSpec(memory_space=pltpu.VMEM)
     anywhere = pl.BlockSpec(memory_space=pl.ANY)
-    results = [
-        jax.ShapeDtypeStruct(array.shape, array.dtype) for array in (layer, grad_input, qkv, out, up)
-    ]
-    results.append(jax.ShapeDtypeStruct((low.shape[0], 2 * low.shape[1]), f32))
+    count = len(arrays)
     return pl.pallas_call(
         finish_kernel,
-        out_shape=[jax.ShapeDtypeStruct((2 * modes, layer.shape[1] // 32), f32)] + results,
-        in_specs=[whole] + [anywhere] * 7,
-        out_specs=[whole] + [anywhere] * 6,
-        scratch_shapes=[
-            pltpu.VMEM(array.shape, array.dtype)
-            for array in (layer, grad_input, qkv, out, up, low, high)
-        ]
-        + [pltpu.SemaphoreType.DMA((7,)), pltpu.SemaphoreType.DMA((7,))],
+        out_shape=[jax.ShapeDtypeStruct((2 * modes, arrays[0].shape[1] // 32), f32)]
+        + [jax.ShapeDtypeStruct(array.shape, array.dtype) for array in arrays],
+        in_specs=[whole] + [anywhere] * count,
+        out_specs=[whole] + [anywhere] * count,
+        scratch_shapes=[pltpu.VMEM(array.shape, array.dtype) for array in arrays]
+        + [pltpu.SemaphoreType.DMA((count,)), pltpu.SemaphoreType.DMA((count,))],
         name="finish",
-    )(share, layer, grad_input, qkv, out, up, low, high)
+    )(share, *arrays)
 
 
 def per_device(
@@ -1535,7 +1634,7 @@
         kv_all,
         o_all,
         lse,
-        returned,
+        out_left,
         attn_sum,
         grad_active,
         weights,
@@ -1543,6 +1642,8 @@
         label_rows,
         cosine,
         sine,
+        qkv_left,
+        both_cotangents,
     ) = attention_forward(
         activations,
         labels.reshape(1, ROWS),
@@ -1553,30 +1654,39 @@
         out_weight,
         down_weight,
     )
-    g_mid, g_low, grad_heads, mlp_part, active_left, gains_two, grad_up, down_low = middle(
+    g_mid, g_low, grad_heads, mlp_part, down_parts, gains_two, grad_up = middle(
         activations,
         attn_sum,
         label_rows,
         norm_gains,
-        cotangent,
+        both_cotangents,
         out_weight,
         grad_active,
         up_weight,
         down_weight,
     )
-    packed, down_high, mlp_sum = attention_backward(
-        grad_heads, q_all, kv_all, o_all, lse, tops, weights, active_left, cotangent, mlp_part
-    )
-    grad_input, layer_out, share, grad_qkv, grad_out = last(
+    packed, grad_down, grad_out, mlp_sum = attention_backward(
+        grad_heads,
+        q_all,
+        kv_all,
+        o_all,
+        lse,
+        tops,
+        weights,
+        down_parts,
+        out_left,
+        g_low,
+        mlp_part,
+    )
+    grad_input, layer_out, share, grad_qkv = last(
         activations,
         label_rows,
         norm_gains,
-        returned,
         packed,
         cosine,
         sine,
         gains_two,
-        g_low,
+        qkv_left,
         attn_sum,
         mlp_sum,
         g_mid,
@@ -1590,8 +1700,7 @@
         grad_qkv,
         grad_out,
         grad_up,
-        down_low,
-        down_high,
+        grad_down,
     )
     return (
         layer_out,

time: 227 us -> 208 us (0.916)
  the two profiles are of different devices: /device:TPU:0 before, /device:TPU:8 now
where the time goes in v1:
time: 208 us; the launch traced here: 204 us
  Pallas kernels  204 us (98%)
    pallas_call x1, Pallas kernels, attention_forward(): pl.pallas_call(forward_kernel, out_shape=[jax.ShapeDtypeStruct((4, ROWS,...  59.8 us
    pallas_call x1, Pallas kernels, attention_backward(): pl.pallas_call(backward_kernel, out_shape=[jax.ShapeDtypeStruct((4, ROWS,...  51.8 us
    pallas_call x1, Pallas kernels, middle(): pl.pallas_call(middle_kernel, out_shape=[jax.ShapeDtypeStruct((ROWS, widt...  45.7 us
    pallas_call x1, Pallas kernels, last(): pl.pallas_call(last_kernel, out_shape=[jax.ShapeDtypeStruct((ROWS, width)...  40.7 us
    pallas_call x1, Pallas kernels, finish(): pl.pallas_call(finish_kernel, out_shape=[jax.ShapeDtypeStruct((2 * modes,...  5.53 us

profile of v1, /device:TPU:8, one launch (start us, length us, event | category | flops | bytes accessed | tf_op | source)
XLA Modules:
  0.0 204.5 jit_solution(9443790125927305504)
XLA Ops:
  0.6 59.8 %attention_forward.1 = (bf16[4,256,128]{2,1,0:T(8,128)(2,1)}, bf16[4,2,4,272,256]{4,3,2,1,0:T(8,128)(2,1)}, f32[1024,128]{1,0:T(8,128)}, f32[8,1024]{1,0:T(8,128...) custom-call(bf16[256,2048]{1,0:T(8,128)(2,1)} %x_ref.5, ...), custom_call_target="tpu_custom_call" | custom-call | tf_op jit(solution)/shard_map/attention_forward/pallas_call | solution.py:806
  60.4 45.7 %middle.1 = (f32[256,2048]{1,0:T(8,128)}, bf16[256,2048]{1,0:T(8,128)(2,1)}, bf16[4,256,128]{2,1,0:T(8,128)(2,1)}, bf16[2,4,64,1024]{3,2,1,0:T(8,128)(2,1)}, bf1...) custom-call(bf16[256,2048]{1,0:T(8,128)(2,1)} %x_ref.5, ...), custom_call_target="tpu_custom_call" | custom-call | tf_op jit(solution)/shard_map/middle/pallas_call | solution.py:1080
  106.1 51.8 %attention_backward.1 = (bf16[4,256,384]{2,1,0:T(8,128)(2,1)}, f32[64,2048]{1,0:T(8,128)}, f32[16,2048]{1,0:T(8,128)}, bf16[2,4,64,1024]{3,2,1,0:T(8,128)(2,1)}) custom-call(bf16[4,256,128]{2,1,0:T(8,128)(2,1)} %get-tuple-element.47.grads, bf16[4,256,128]{2,1,0:T(8,128)(2,1)} %get-tuple-element.48.q_ref, ...), custom_call_target="tpu_custom_call" | custom-call | tf_op jit(solution)/shard_map/attention_backward/pallas_call | solution.py:1333
  158.0 40.7 %last.1 = (f32[256,2048]{1,0:T(8,128)}, bf16[256,2048]{1,0:T(8,128)(2,1)}, f32[8,128]{1,0:T(8,128)}, f32[3,64,512]{2,1,0:T(8,128)}) custom-call(bf16[256,2048]{1,0:T(8,128)(2,1)} %x_ref.5, s32[256,128]{1,0:T(8,128)} %get-tuple-element.43.labels_ref, f32[6,2048]{1,0:T(8,128)} %gains_ref.5, bf16[4,256,384]{2,1,0:T(8,128)(2,1)} %get-tuple-element.58.packed_ref, ...), custom_call_target="tpu_custom_call" | custom-call | tf_op jit(solution)/shard_map/last/pallas_call | solution.py:1528
  198.7 5.5 %finish.1 = (f32[6,64]{1,0:T(8,128)}, bf16[256,2048]{1,0:T(8,128)(2,1)}, f32[256,2048]{1,0:T(8,128)}, f32[3,64,512]{2,1,0:T(8,128)}, f32[16,2048]{1,0:T(8,128)}, /*index=5*/f32[64,2048]{1,0:T(8,128)}, f32[64,2048]{1,0:T(8,128)}) custom-call(f32[8,128]{1,0:T(8,128)} %get-tuple-element.65.share_ref, bf16[256,2048]{1,0:T(8,128)(2,1)} %get-tuple-element.66.layer_in, ...), custom_call_target="tpu_custom_call" | custom-call | tf_op jit(solution)/shard_map/finish/pallas_call | solution.py:1608

commit v2 on v1

--- a/solution.py
+++ b/solution.py
@@ -283,11 +283,21 @@
     def fill(group, step):
         at = spot(ways[group], step)
         value = partial_block(both_left, both_right, ways[group], at, group, width)
-        if by_rows:
-            parts[group, at] = value.reshape((2,) + first_shape)
-        else:
+        parts[group, at] = value.reshape((2,) + first_shape)
+
+    def fill_all(group):
+        tall = both_left[...].reshape(16 * rows, 2 * ROWS)
+        value = dot(tall, both_right[:, group * width : (group + 1) * width]).astype(bf16)
+        for at in range(4):
+            if ways[group] == 0:
+                block = value[at * 4 * rows : (at + 1) * 4 * rows]
+            else:
+                block = jnp.concatenate(
+                    [value[(k * 4 + at) * rows : (k * 4 + at + 1) * rows] for k in range(4)],
+                    axis=0,
+                )
             for half_index in range(2):
-                parts[group, at, half_index] = value[
+                parts[group, at, half_index] = block[
                     :, half_index * first_shape[1] : (half_index + 1) * first_shape[1]
                 ]
 
@@ -303,9 +313,11 @@
             continue
         if ready is not None:
             ready(group)
-        if parts_hbm is None:
+        if parts_hbm is None and by_rows:
             for step in (2, 1, -1):
                 fill(group, step)
+        elif parts_hbm is None:
+            fill_all(group)
         first_done[group] = []
         first[group] = ring_sum(
             copies,
@@ -317,7 +329,7 @@
         )
         next(first[group])
         yield
-    if parts_hbm is None:
+    if parts_hbm is None and by_rows:
         for group in range(groups):
             fill(group, 0)
     for wait in waits:
@@ -443,12 +455,15 @@
 
 
 def query_bounds(keys_values, z, core, bounds):
+    size = ROWS // 2
     for n in range(4):
         digits = keys_values[z, core, n, ROWS:, :].astype(f32)
         code = (digits[0:1] * 128.0 + digits[1:2]).astype(jnp.int32)
         low = jnp.where(code >= CLIP_STEP, CLIP_STEP, 0)
-        bounds[0:1, n * ROWS : (n + 1) * ROWS] = low
-        bounds[1:2, n * ROWS : (n + 1) * ROWS] = code - low
+        for half in range(2):
+            at = slice((half * 4 + n) * size, (half * 4 + n + 1) * size)
+            bounds[0:1, at] = low[:, half * size : (half + 1) * size]
+            bounds[1:2, at] = (code - low)[:, half * size : (half + 1) * size]
 
 
 def forward_kernel(
@@ -565,18 +580,18 @@
     send_kv(1)
     query_part = dot(normed[...], weight[0]) * (HD**-0.5 / math.log(2.0))
     for head in range(4):
-        q_own[head] = rotate(query_part, head).astype(bf16)
+        q_own[head] = rotate(query_part, head).astype(bf16).reshape(2, ROWS // 2, HD)
     for n, hop in enumerate(HOPS):
         other = around(x, hop)
         q_came[n] = copies.start(
             q_own.at[other],
-            queries.at[x],
+            queries.at[:, x],
             device(other, y, z, core),
-            queries.at[around(x, -hop)],
+            queries.at[:, around(x, -hop)],
         )
     send_kv(2)
     keys_values[z, core, x] = kv_own[x]
-    queries[x] = q_own[x]
+    queries[:, x] = q_own[x]
     above, below = device(x, y, around(z, 1), core), device(x, y, around(z, -1), core)
     next_z, last_z, far_z = around(z, 1), around(z, -1), around(z, 2)
     pieces = [x] + [around(x, -hop) for hop in HOPS]
@@ -632,34 +647,41 @@
         arrival.wait_recv()
     query_bounds(keys_values, z, core, bounds_ref)
 
-    stored = []
-
-    def attend(z_at, core_at):
-        count = len(stored)
-        column[...] = key_column(keys_values, z_at, core_at)
-        query = queries[...].reshape(4 * ROWS, HD)
+    stored, chunks = {}, []
+
+    def attend_half(count, half):
+        z_at, core_at = chunks[count]
+        at = slice(half * 2 * ROWS, (half + 1) * 2 * ROWS)
+        if half == 0:
+            column[count % 2] = key_column(keys_values, z_at, core_at)
+        query = queries[half].reshape(2 * ROWS, HD)
         keys = keys_values[z_at, core_at, :, :ROWS, :HD].reshape(4 * ROWS, HD)
         values = keys_values[z_at, core_at, :, :ROWS, HD:].reshape(4 * ROWS, HD)
         scores = dot(keys, query, NT)
-        codes = jnp.concatenate([column[...]] * (4 * ROWS // HD), axis=1)
-        seen = visible(codes, bounds_ref[0:1, :], bounds_ref[1:2, :])
+        codes = jnp.concatenate([column[count % 2]] * (2 * ROWS // HD), axis=1)
+        seen = visible(codes, bounds_ref[0:1, at], bounds_ref[1:2, at])
         scores = jnp.where(seen, scores, -1e30)
-        top_before = top[0:1, :]
+        top_before = top[0:1, at]
         top_now = jnp.maximum(top_before, jnp.max(scores, axis=0, keepdims=True))
         if count >= 2:
-            stored[count - 2].wait()
-        slot = weights.at[count % 2]
+            stored[count - 2, half].wait()
+        slot = weights.at[count % 2, half]
         slot[...] = jnp.exp2(scores - top_now).astype(bf16)
         shrink = jnp.exp2(top_before - top_now)
-        norm[...] = norm[...] * shrink + dot(jnp.ones((8, 4 * ROWS), bf16), slot[...])
-        top[0:1, :] = top_now
-        acc[...] = acc[...] * shrink + dot(values, slot[...], TN)
-        tops_ref[z_at, core_at] = jnp.broadcast_to(top_now, tops_ref.shape[2:])
+        norm[:, at] = norm[:, at] * shrink + dot(jnp.ones((8, 4 * ROWS), bf16), slot[...])
+        top[0:1, at] = top_now
+        acc[:, at] = acc[:, at] * shrink + dot(values, slot[...], TN)
+        tops_ref[z_at, core_at, :, at] = jnp.broadcast_to(top_now, (8, 2 * ROWS))
         copy = pltpu.make_async_copy(
-            slot, weights_ref.at[z_at, core_at], weight_sems.at[count % 2]
+            slot, weights_ref.at[z_at, core_at, half], weight_sems.at[count % 2, half]
         )
         copy.start()
-        stored.append(copy)
+        stored[count, half] = copy
+
+    def attend(z_at, core_at):
+        chunks.append((z_at, core_at))
+        for half in range(2):
+            attend_half(len(chunks) - 1, half)
 
     low_far, high_far, twin_last, twin_next = [], [], [], []
 
@@ -716,54 +738,80 @@
     take(twin_next)
     attend(next_z, 1 - core)
     w_onward(3)
-    attend(far_z, core)
+    size = ROWS // 2
+    came_back = {}
+
+    def give_back(half):
+        at = slice(half * 2 * ROWS, (half + 1) * 2 * ROWS)
+        total_norm = norm[0:1, at]
+        attended = (acc[:, at] / total_norm).T
+        o_low[half] = attended.astype(bf16).reshape(4, size, HD)
+        came_back[half] = [
+            copies.start(
+                o_low.at[half, around(x, hop)],
+                back.at[half, x],
+                device(around(x, hop), y, z, core),
+                back.at[half, around(x, -hop)],
+            )
+            for hop in HOPS
+        ]
+        back[half, x] = o_low[half, x]
+        o_ref[at, :] = attended
+        lse_ref[:, at] = jnp.broadcast_to(top[0:1, at] + jnp.log2(total_norm), (8, 2 * ROWS))
+
+    ring_last, ring_next, ring_low, ring_high = [], [], [], []
+
+    def spread_y(half):
+        take(came_back[half])
+        for n in range(4):
+            gathered[y, half, :, n * HD : (n + 1) * HD] = back[half, n]
+        block = gathered.at[y, half]
+        ring_last.append(copies.start(block, block, y_up, gathered.at[y_last, half]))
+        ring_next.append(copies.start(block, block, y_down, gathered.at[y_next, half]))
+
+    def onward_y(half):
+        low, high = pl.ds(0, size // 2), pl.ds(size // 2, size // 2)
+        ring_last[half].wait_recv()
+        block = gathered.at[y_last, half, low]
+        ring_low.append(copies.start(block, block, y_up, gathered.at[y_far, half, low]))
+        ring_next[half].wait_recv()
+        block = gathered.at[y_next, half, high]
+        ring_high.append(copies.start(block, block, y_down, gathered.at[y_far, half, high]))
+
+    chunks += [(far_z, core), (far_z, 1 - core)]
+    attend_half(6, 0)
     take(twin_far)
+    attend_half(7, 0)
+    give_back(0)
+    attend_half(6, 1)
+    spread_y(0)
+    attend_half(7, 1)
+    give_back(1)
     keep = pltpu.make_async_copy(keys_values, kv_all_ref, load_sems.at[2])
     keep.start()
-    attend(far_z, 1 - core)
-
-    total_norm = norm[0:1, :]
-    attended = (acc[...] / total_norm).T
-    o_low[...] = attended.astype(bf16).reshape(4, ROWS, HD)
-    came_back = []
-    for hop in HOPS:
-        other = around(x, hop)
-        came_back.append(
-            copies.start(
-                o_low.at[other],
-                back.at[x],
-                device(other, y, z, core),
-                back.at[around(x, -hop)],
-            )
-        )
-    back[x] = o_low[x]
-    o_ref[...] = attended
-    lse_ref[...] = jnp.broadcast_to(top[0:1, :] + jnp.log2(total_norm), lse_ref.shape)
     q_all_ref[...] = queries[...]
     for n in range(4):
         w_far[n].wait_recv()
         block = out_weight.at[y_far, core, n]
         w_twin.append(copies.start(block, block, twin, out_weight.at[y_far, 1 - core, n]))
-    take(came_back)
     local = 4 * HD
-    for n in range(4):
-        gathered[y, :, n * HD : (n + 1) * HD] = back[n]
-    half = ROWS // 2
-    block = gathered.at[y]
-    ring_last = copies.start(block, block, y_up, gathered.at[y_last])
-    ring_next = copies.start(block, block, y_down, gathered.at[y_next])
+    spread_y(1)
     out_rows = out_left_ref.shape[2]
     for core_at in range(2):
-        out_left_ref[:, core_at] = pick(core_at, gathered[y], out_rows, 0).reshape(
-            16, out_rows, ROWS
-        )
+        out_left_ref[:, core_at] = pick(
+            core_at, gathered[y].reshape(ROWS, local), out_rows, 0
+        ).reshape(16, out_rows, ROWS)
     keep_grad.wait()
     summed = grad_active_ref
 
     def project(index, owners, first, final):
         at = slab(index, WIDE)
         part = sum(
-            dot(gathered[n], out_weight[n, :, :, :, at].reshape(local, WIDE)) for n in owners
+            dot(
+                gathered[n].reshape(ROWS, local),
+                out_weight[n, :, :, :, at].reshape(local, WIDE),
+            )
+            for n in owners
         )
         if not first:
             part = part + summed[:, at]
@@ -775,23 +823,19 @@
     count = total_ref.shape[1] // WIDE
     steps(count, lambda index: project(index, (y,), True, False))
     take(w_twin)
-    ring_last.wait_recv()
-    block = gathered.at[y_last, pl.ds(0, half)]
-    ring_low = copies.start(block, block, y_up, gathered.at[y_far, pl.ds(0, half)])
-    ring_next.wait_recv()
-    block = gathered.at[y_next, pl.ds(half, half)]
-    ring_high = copies.start(block, block, y_down, gathered.at[y_far, pl.ds(half, half)])
+    onward_y(0)
+    onward_y(1)
     steps(count, lambda index: project(index, (y_last, y_next), False, False))
-    ring_low.wait_recv()
-    ring_high.wait_recv()
+    take(ring_low + ring_high)
     steps(count, lambda index: project(index, (y_far,), False, True))
     copies.finish()
     keep.wait()
     for copy in keep_more:
         copy.wait()
     take(for_twin)
-    for copy in stored[-2:]:
-        copy.wait()
+    for count in (6, 7):
+        for half in range(2):
+            stored[count, half].wait()
 
 
 def attention_forward(
@@ -800,20 +844,20 @@
     width = out_weight.shape[1]
     whole = pl.BlockSpec(memory_space=pltpu.VMEM)
     anywhere = pl.BlockSpec(memory_space=pl.ANY)
-    count = 3 + 3 + 12 + 16 + 4 + 3 + 4 + 8 + 4 + 8 + 4 + 2
+    count = 3 + 3 + 12 + 16 + 4 + 6 + 8 + 8 + 4 + 8 + 4 + 2
     local = out_weight.shape[0]
     pieces = (2, 4, out_weight.shape[0] // 8, width)
     return pl.pallas_call(
         forward_kernel,
         out_shape=[
-            jax.ShapeDtypeStruct((4, ROWS, HD), bf16),
+            jax.ShapeDtypeStruct((2, 4, ROWS // 2, HD), bf16),
             jax.ShapeDtypeStruct((4, 2, 4, ROWS + CODE_ROWS, 2 * HD), bf16),
             jax.ShapeDtypeStruct((4 * ROWS, HD), f32),
             jax.ShapeDtypeStruct((8, 4 * ROWS), f32),
             jax.ShapeDtypeStruct((16, 2, local // 32, ROWS), bf16),
             jax.ShapeDtypeStruct((ROWS, width), bf16),
             jax.ShapeDtypeStruct((ROWS, down_weight.shape[0]), f32),
-            jax.ShapeDtypeStruct((4, 2, 4 * ROWS, 4 * ROWS), bf16),
+            jax.ShapeDtypeStruct((4, 2, 2, 4 * ROWS, 2 * ROWS), bf16),
             jax.ShapeDtypeStruct((4, 2, 8, 4 * ROWS), f32),
             jax.ShapeDtypeStruct((ROWS, HD), jnp.int32),
             jax.ShapeDtypeStruct((ROWS, HD), f32),
@@ -834,24 +878,24 @@
             pltpu.VMEM(weight.shape, bf16),
             pltpu.VMEM((4,) + pieces, bf16),
             pltpu.VMEM(down_weight.shape, bf16),
-            pltpu.VMEM((2, 4 * ROWS, 4 * ROWS), bf16),
+            pltpu.VMEM((2, 2, 4 * ROWS, 2 * ROWS), bf16),
             pltpu.VMEM(activations.shape, bf16),
-            pltpu.VMEM((4, ROWS, HD), bf16),
+            pltpu.VMEM((4, 2, ROWS // 2, HD), bf16),
             pltpu.VMEM((4, ROWS + CODE_ROWS, 2 * HD), bf16),
-            pltpu.VMEM((4, ROWS, HD), bf16),
+            pltpu.VMEM((2, 4, ROWS // 2, HD), bf16),
             pltpu.VMEM((4, 2, 4, ROWS + CODE_ROWS, 2 * HD), bf16),
             pltpu.VMEM((8, 4 * ROWS), f32),
             pltpu.VMEM((8, 4 * ROWS), f32),
             pltpu.VMEM((HD, 4 * ROWS), f32),
-            pltpu.VMEM((4 * ROWS, HD), jnp.int32),
+            pltpu.VMEM((2, 4 * ROWS, HD), jnp.int32),
             pltpu.VMEM((8, 4 * ROWS), jnp.int32),
-            pltpu.VMEM((4, ROWS, HD), bf16),
-            pltpu.VMEM((4, ROWS, HD), bf16),
-            pltpu.VMEM((4, ROWS, 4 * HD), bf16),
+            pltpu.VMEM((2, 4, ROWS // 2, HD), bf16),
+            pltpu.VMEM((2, 4, ROWS // 2, HD), bf16),
+            pltpu.VMEM((4, 2, ROWS // 2, 4 * HD), bf16),
             pltpu.SemaphoreType.DMA((count,)),
             pltpu.SemaphoreType.DMA((count,)),
             pltpu.SemaphoreType.DMA((7,)),
-            pltpu.SemaphoreType.DMA((2,)),
+            pltpu.SemaphoreType.DMA((2, 2)),
         ],
         compiler_params=pltpu.CompilerParams(
             collective_id=0, has_side_effects=True, vmem_limit_bytes=VMEM_LIMIT
@@ -1039,18 +1083,18 @@
     steps(ROWS // NORM_ROWS, back)
     by_head = dot(g_low[...], out_weight[...], NT).astype(bf16)
     for head in range(4):
-        g_heads[head] = by_head[:, head * HD : (head + 1) * HD]
+        g_heads[head] = by_head[:, head * HD : (head + 1) * HD].reshape(2, ROWS // 2, HD)
     x_copies = Copies(x_send, x_recv)
     arrivals = [
         x_copies.start(
             g_heads.at[around(x, hop)],
-            heads_ref.at[x],
+            heads_ref.at[:, x],
             device(around(x, hop), y, z, core),
-            heads_ref.at[around(x, -hop)],
+            heads_ref.at[:, around(x, -hop)],
         )
         for hop in HOPS
     ]
-    heads_ref[x] = g_heads[x]
+    heads_ref[:, x] = g_heads[x]
     keep += [move(g_mid, g_mid_hbm), move(g_low, g_low_hbm)]
     advance(ring)
     fill_down(2)
@@ -1082,7 +1126,7 @@
         out_shape=[
             jax.ShapeDtypeStruct((ROWS, width), f32),
             jax.ShapeDtypeStruct((ROWS, width), bf16),
-            jax.ShapeDtypeStruct((4, ROWS, HD), bf16),
+            jax.ShapeDtypeStruct((2, 4, ROWS // 2, HD), bf16),
             jax.ShapeDtypeStruct(summed, bf16),
             jax.ShapeDtypeStruct(down_parts, bf16),
             jax.ShapeDtypeStruct((8, width), f32),
@@ -1109,7 +1153,7 @@
         + [
             pltpu.VMEM(down_parts, bf16),
             pltpu.VMEM(summed, bf16),
-            pltpu.VMEM((4, ROWS, HD), bf16),
+            pltpu.VMEM((4, 2, ROWS // 2, HD), bf16),
         ]
         + sum_scratch(width)
         + [pltpu.SemaphoreType.DMA((12,))]
@@ -1135,9 +1179,9 @@
 
 
 def backward_kernel(
-    grads, q_ref, kv_hbm, o_ref, lse_ref, tops_ref, weights_hbm, down_parts_hbm, out_left_hbm, g_low_hbm, given_ref,
-    packed_ref, grad_down_ref, grad_out_ref, total_ref,
-    keys_values, weights, delta, grad_q, parts, met, came, sums, q_low, back_q,
+    grads, q_ref, kv_hbm, o_ref, lse_ref, tops_ref, weights_hbm, down_parts_hbm, out_left_hbm, g_low_hbm, given_hbm,
+    packed_ref, grad_down_ref, grad_out_ref, total_hbm,
+    given_ref, keys_values, weights, delta, grad_q, parts, met, came, sums, q_low, back_q,
     back_kv, send_sems, recv_sems, load_sems, weight_sems, y_came, all_rows, y_send, y_recv, *more,
 ):
     here = place()
@@ -1155,8 +1199,6 @@
         for at in (far_z, next_z, last_z, z)
         for core_at in (1 - core, core)
     ]
-    load = pltpu.make_async_copy(kv_hbm, keys_values, load_sems.at[0])
-    load.start()
 
     def fetch(index):
         copy = pltpu.make_async_copy(
@@ -1167,7 +1209,19 @@
         copy.start()
         return copy
 
-    fetched = [fetch(0), fetch(1)]
+    load_given = pltpu.make_async_copy(given_hbm, given_ref, load_sems.at[8])
+    load_given.start()
+    fetched = [fetch(0)]
+    loads = []
+    for n, (z_at, core_at) in enumerate(order):
+        loads.append(
+            pltpu.make_async_copy(
+                kv_hbm.at[z_at, core_at], keys_values.at[z_at, core_at], load_sems.at[n]
+            )
+        )
+        loads[n].start()
+        if n == 0:
+            fetched.append(fetch(1))
     copies = Copies(send_sems, recv_sems)
     y_copies = Copies(y_send, y_recv)
     over_y = [
@@ -1180,6 +1234,7 @@
     )
     arrived()
     advance(ring, 5)
+    load_given.wait()
     for half in over_y:
         advance(half)
     advance(ring_out)
@@ -1188,7 +1243,6 @@
     delta[...] = lax.dot_general(
         jnp.ones((8, HD), f32), product, NT, preferred_element_type=f32, precision=highest
     )
-    load.wait()
     done = []
 
     def chunk(z_at, core_at):
@@ -1196,20 +1250,24 @@
         done.append(index)
         if index + 2 < len(order):
             fetched.append(fetch(index + 2))
+        loads[index].wait()
         fetched[index].wait()
-        slot = weights.at[index % 3]
-        query = q_ref[...].reshape(4 * ROWS, HD)
-        grad = grads[...].reshape(4 * ROWS, HD)
         keys = keys_values[z_at, core_at, :, :ROWS, :HD].reshape(4 * ROWS, HD)
         values = keys_values[z_at, core_at, :, :ROWS, HD:].reshape(4 * ROWS, HD)
-        rescale = jnp.exp2(tops_ref[z_at, core_at, 0:1, :] - lse_ref[0:1, :])
-        grad_weights = dot(values, grad, NT)
-        taken = slot[...].astype(f32) * rescale
-        slot[...] = taken.astype(bf16)
-        grad_v = dot(slot[...], grad)
-        slot[...] = (taken * (grad_weights - delta[0:1, :])).astype(bf16)
-        grad_k = dot(slot[...], query)
-        grad_q[...] += dot(keys, slot[...], TN)
+        grad_k = grad_v = 0.0
+        for half in range(2):
+            at = slice(half * 2 * ROWS, (half + 1) * 2 * ROWS)
+            slot = weights.at[index % 3, half]
+            query = q_ref[half].reshape(2 * ROWS, HD)
+            grad = grads[half].reshape(2 * ROWS, HD)
+            rescale = jnp.exp2(tops_ref[z_at, core_at, 0:1, at] - lse_ref[0:1, at])
+            grad_weights = dot(values, grad, NT)
+            taken = slot[...].astype(f32) * rescale
+            slot[...] = taken.astype(bf16)
+            grad_v += dot(slot[...], grad)
+            slot[...] = (taken * (grad_weights - delta[0:1, at])).astype(bf16)
+            grad_k += dot(slot[...], query)
+            grad_q[:, at] += dot(keys, slot[...], TN)
         parts[z_at, core_at] = (
             jnp.concatenate([grad_k * math.log(2.0), grad_v], axis=1)
             .astype(bf16)
@@ -1269,19 +1327,19 @@
     advance(ring)
     advance(ring_out)
     chunk(z, core)
-    q_low[...] = (grad_q[...] * (HD**-0.5)).T.astype(bf16).reshape(4, ROWS, HD)
+    q_low[...] = (grad_q[...] * (HD**-0.5)).T.astype(bf16).reshape(2, 4, ROWS // 2, HD)
     arrivals = []
     for hop in HOPS:
         other = around(x, hop)
         arrivals.append(
             copies.start(
-                q_low.at[other],
+                q_low.at[:, other],
                 back_q.at[x],
                 device(other, y, z, core),
                 back_q.at[around(x, -hop)],
             )
         )
-    back_q[x] = q_low[x]
+    back_q[x] = q_low[:, x]
     advance(ring)
     advance(ring_out, 2)
     own_met.wait_recv()
@@ -1307,7 +1365,8 @@
     back_kv[x] = sums[x]
     for half in over_y:
         advance(half)
-    total_ref[...] = all_rows[...]
+    keep = pltpu.make_async_copy(all_rows, total_hbm, load_sems.at[9])
+    keep.start()
     advance(ring)
     advance(ring_out, 2)
     advance(ring)
@@ -1316,8 +1375,9 @@
     for arrival in arrivals:
         arrival.wait_recv()
     for n in range(4):
-        packed_ref[n, :, :HD] = back_q[n]
+        packed_ref[n, :, :HD] = back_q[n].reshape(ROWS, HD)
         packed_ref[n, :, HD:] = back_kv[n]
+    keep.wait()
     copies.finish()
     y_copies.finish()
 
@@ -1338,23 +1398,24 @@
             jax.ShapeDtypeStruct((out_rows, width), f32),
             jax.ShapeDtypeStruct(given.shape, bf16),
         ],
-        in_specs=[whole, whole, anywhere] + [whole] * 3 + [anywhere] * 4 + [whole],
-        out_specs=[whole] * 4,
+        in_specs=[whole, whole, anywhere] + [whole] * 3 + [anywhere] * 5,
+        out_specs=[whole] * 3 + [anywhere],
         scratch_shapes=[
+            pltpu.VMEM(given.shape, bf16),
             pltpu.VMEM((4, 2, 4, ROWS + CODE_ROWS, 2 * HD), bf16),
-            pltpu.VMEM((3, 4 * ROWS, 4 * ROWS), bf16),
+            pltpu.VMEM((3, 2, 4 * ROWS, 2 * ROWS), bf16),
             pltpu.VMEM((8, 4 * ROWS), f32),
             pltpu.VMEM((HD, 4 * ROWS), f32),
             pltpu.VMEM((4, 2, 2, 2 * ROWS, 2 * HD), bf16),
             pltpu.VMEM((4, 2, 2 * ROWS, 2 * HD), bf16),
             pltpu.VMEM((6, 2 * ROWS, 2 * HD), bf16),
             pltpu.VMEM((4, ROWS, 2 * HD), bf16),
-            pltpu.VMEM((4, ROWS, HD), bf16),
-            pltpu.VMEM((4, ROWS, HD), bf16),
+            pltpu.VMEM((2, 4, ROWS // 2, HD), bf16),
+            pltpu.VMEM((4, 2, ROWS // 2, HD), bf16),
             pltpu.VMEM((4, ROWS, 2 * HD), bf16),
             pltpu.SemaphoreType.DMA((count,)),
             pltpu.SemaphoreType.DMA((count,)),
-            pltpu.SemaphoreType.DMA((1,)),
+            pltpu.SemaphoreType.DMA((10,)),
             pltpu.SemaphoreType.DMA((3,)),
         ]
         + sum_scratch(2 * given.shape[3])
@@ -1373,8 +1434,8 @@
 def last_kernel(
     x_ref, labels_ref, gains_ref, packed_ref, cos_ref, sin_ref, gains_two_ref, left_hbm, attn_hbm, mlp_hbm, g_mid_hbm,
     weight_hbm,
-    input_ref, layer_ref, gains_out_ref, grad_qkv_ref,
-    attn, mlp, g_mid, weight, xhat, inverse, given, gains_part, gains_given, came, all_rows, y_send, y_recv, load_sems,
+    input_hbm, layer_hbm, gains_out_ref, grad_qkv_ref,
+    input_ref, layer_ref, attn, mlp, g_mid, weight, xhat, inverse, given, gains_part, gains_given, came, all_rows, y_send, y_recv, load_sems,
     qkv_left, qkv_right, *more,
 ):
     gain_scratch = more[: len(GAIN_SCRATCH)]
@@ -1489,13 +1550,17 @@
         layer_ref[at, :] = total.astype(bf16)
 
     steps(ROWS // NORM_ROWS, finish_layer)
+    keep = [pltpu.make_async_copy(layer_ref, layer_hbm, load_sems.at[5])]
+    keep[0].start()
     advance(over_y[0])
     advance(over_all)
     advance(ring)
     advance(over_y[1])
-    advance(over_y[0])
+    advance(over_all)
     advance(ring)
     advance(over_all)
+    advance(ring)
+    advance(over_y[0])
     advance(over_y[1])
 
     def finish_input(index):
@@ -1506,12 +1571,17 @@
         along = jnp.mean(grad * unit, axis=-1, keepdims=True)
         input_ref[at, :] = g_mid[at, :] + inverse[at, :1] * (grad - mean - unit * along)
 
-    steps(ROWS // NORM_ROWS, finish_input)
-    advance(ring)
+    for half in range(2):
+        steps(norm_steps, lambda index: finish_input(index + half * norm_steps))
+        at = pl.ds(half * (ROWS // 2), ROWS // 2)
+        keep.append(
+            pltpu.make_async_copy(input_ref.at[at], input_hbm.at[at], load_sems.at[6 + half])
+        )
+        keep[-1].start()
+        advance(ring)
     advance(over_all)
-    advance(ring)
-    advance(over_all)
-    advance(ring)
+    for copy in keep:
+        copy.wait()
     copies.finish()
     gain_copies.finish()
 
@@ -1534,8 +1604,10 @@
             jax.ShapeDtypeStruct((3, rows, local), f32),
         ],
         in_specs=[whole] * 7 + [anywhere] * 5,
-        out_specs=[whole] * 4,
+        out_specs=[anywhere] * 2 + [whole] * 2,
         scratch_shapes=[
+            pltpu.VMEM((ROWS, width), f32),
+            pltpu.VMEM((ROWS, width), bf16),
             pltpu.VMEM(attn_sum.shape, bf16),
             pltpu.VMEM(mlp_sum.shape, bf16),
             pltpu.VMEM(g_mid.shape, f32),
@@ -1547,7 +1619,7 @@
             pltpu.VMEM((4, 4, 2, 8, HD), f32),
         ]
         + sum_scratch(width)
-        + [pltpu.SemaphoreType.DMA((5,))]
+        + [pltpu.SemaphoreType.DMA((8,))]
         + factor_scratch(rows, cols)
         + [pltpu.VMEM(shape, f32) for shape in GAIN_SCRATCH]
         + [pltpu.SemaphoreType.DMA((10,)), pltpu.SemaphoreType.DMA((10,))]

time: 208 us -> 206 us (level)
  the two profiles are of different devices: /device:TPU:8 before, /device:TPU:0 now
where the time goes in v2:
time: 206 us; the launch traced here: 202 us
  Pallas kernels  201 us (98%)
    pallas_call x1, Pallas kernels, attention_forward(): pl.pallas_call(forward_kernel, out_shape=[jax.ShapeDtypeStruct((2, 4, ROW...  61.8 us
    pallas_call x1, Pallas kernels, attention_backward(): pl.pallas_call(backward_kernel, out_shape=[jax.ShapeDtypeStruct((4, ROWS,...  50.8 us
    pallas_call x1, Pallas kernels, middle(): pl.pallas_call(middle_kernel, out_shape=[jax.ShapeDtypeStruct((ROWS, widt...  46.1 us
    pallas_call x1, Pallas kernels, last(): pl.pallas_call(last_kernel, out_shape=[jax.ShapeDtypeStruct((ROWS, width)...  36.3 us
    pallas_call x1, Pallas kernels, finish(): pl.pallas_call(finish_kernel, out_shape=[jax.ShapeDtypeStruct((2 * modes,...  5.53 us

profile of v2, /device:TPU:0, one launch (start us, length us, event | category | flops | bytes accessed | tf_op | source)
XLA Modules:
  0.0 201.6 jit_solution(8037749860518513504)
XLA Ops:
  0.6 61.8 %attention_forward.1 = (bf16[2,4,128,128]{3,2,1,0:T(8,128)(2,1)}, bf16[4,2,4,272,256]{4,3,2,1,0:T(8,128)(2,1)}, f32[1024,128]{1,0:T(8,128)}, f32[8,1024]{1,0:T(8...) custom-call(bf16[256,2048]{1,0:T(8,128)(2,1)} %x_ref.5, ...), custom_call_target="tpu_custom_call" | custom-call | tf_op jit(solution)/shard_map/attention_forward/pallas_call | solution.py:850
  62.5 46.1 %middle.1 = (f32[256,2048]{1,0:T(8,128)}, bf16[256,2048]{1,0:T(8,128)(2,1)}, bf16[2,4,128,128]{3,2,1,0:T(8,128)(2,1)}, bf16[2,4,64,1024]{3,2,1,0:T(8,128)(2,1)},...) custom-call(bf16[256,2048]{1,0:T(8,128)(2,1)} %x_ref.5, ...), custom_call_target="tpu_custom_call" | custom-call | tf_op jit(solution)/shard_map/middle/pallas_call | solution.py:1124
  108.6 50.8 %attention_backward.1 = (bf16[4,256,384]{2,1,0:T(8,128)(2,1)}, f32[64,2048]{1,0:T(8,128)}, f32[16,2048]{1,0:T(8,128)}, bf16[2,4,64,1024]{3,2,1,0:T(8,128)(2,1)}) custom-call(bf16[2,4,128,128]{3,2,1,0:T(8,128)(2,1)} %get-tuple-element.47.grads, bf16[2,4,128,128]{3,2,1,0:T(8,128)(2,1)} %get-tuple-element.48.q_ref, ...), custom_call_target="tpu_custom_call" | custom-call | tf_op jit(solution)/shard_map/attention_backward/pallas_call | solution.py:1393
  159.4 36.3 %last.1 = (f32[256,2048]{1,0:T(8,128)}, bf16[256,2048]{1,0:T(8,128)(2,1)}, f32[8,128]{1,0:T(8,128)}, f32[3,64,512]{2,1,0:T(8,128)}) custom-call(bf16[256,2048]{1,0:T(8,128)(2,1)} %x_ref.5, s32[256,128]{1,0:T(8,128)} %get-tuple-element.43.labels_ref, f32[6,2048]{1,0:T(8,128)} %gains_ref.5, bf16[4,256,384]{2,1,0:T(8,128)(2,1)} %get-tuple-element.58.packed_ref, ...), custom_call_target="tpu_custom_call" | custom-call | tf_op jit(solution)/shard_map/last/pallas_call | solution.py:1598
  195.7 5.5 %finish.1 = (f32[6,64]{1,0:T(8,128)}, bf16[256,2048]{1,0:T(8,128)(2,1)}, f32[256,2048]{1,0:T(8,128)}, f32[3,64,512]{2,1,0:T(8,128)}, f32[16,2048]{1,0:T(8,128)}, /*index=5*/f32[64,2048]{1,0:T(8,128)}, f32[64,2048]{1,0:T(8,128)}) custom-call(f32[8,128]{1,0:T(8,128)} %get-tuple-element.65.share_ref, bf16[256,2048]{1,0:T(8,128)(2,1)} %get-tuple-element.66.layer_in, ...), custom_call_target="tpu_custom_call" | custom-call | tf_op jit(solution)/shard_map/finish/pallas_call | solution.py:1680

commit v3 on v2

--- a/solution.py
+++ b/solution.py
@@ -1179,8 +1179,8 @@
 
 
 def backward_kernel(
-    grads, q_ref, kv_hbm, o_ref, lse_ref, tops_ref, weights_hbm, down_parts_hbm, out_left_hbm, g_low_hbm, given_hbm,
-    packed_ref, grad_down_ref, grad_out_ref, total_hbm,
+    grads, q_ref, kv_hbm, o_ref, lse_ref, tops_ref, weights_hbm, down_parts_hbm, given_hbm,
+    packed_ref, grad_down_ref, total_hbm,
     given_ref, keys_values, weights, delta, grad_q, parts, met, came, sums, q_low, back_q,
     back_kv, send_sems, recv_sems, load_sems, weight_sems, y_came, all_rows, y_send, y_recv, *more,
 ):
@@ -1229,15 +1229,11 @@
         for half in range(2)
     ]
     ring = weight_grad(here, grad_down_ref, more[:7], parts_hbm=down_parts_hbm, ways=DOWN_WAYS)
-    ring_out = weight_grad(
-        here, grad_out_ref, more[9:], more[7:9], left=out_left_hbm, right=g_low_hbm
-    )
     arrived()
     advance(ring, 5)
     load_given.wait()
     for half in over_y:
         advance(half)
-    advance(ring_out)
     grad_q[...] = jnp.zeros_like(grad_q)
     product = grads[...].reshape(4 * ROWS, HD).astype(f32) * o_ref[...]
     delta[...] = lax.dot_general(
@@ -1287,7 +1283,6 @@
     above, below = device(x, y, next_z, core), device(x, y, last_z, core)
     chunk(far_z, 1 - core)
     far_met = hand_over(far_z)
-    advance(ring_out, 5)
     chunk(far_z, core)
     chunk(next_z, 1 - core)
     next_met = hand_over(next_z)
@@ -1325,7 +1320,6 @@
     for half in over_y:
         advance(half)
     advance(ring)
-    advance(ring_out)
     chunk(z, core)
     q_low[...] = (grad_q[...] * (HD**-0.5)).T.astype(bf16).reshape(2, 4, ROWS // 2, HD)
     arrivals = []
@@ -1341,7 +1335,6 @@
         )
     back_q[x] = q_low[:, x]
     advance(ring)
-    advance(ring_out, 2)
     own_met.wait_recv()
     raw_last.wait_recv()
     raw_next.wait_recv()
@@ -1368,9 +1361,7 @@
     keep = pltpu.make_async_copy(all_rows, total_hbm, load_sems.at[9])
     keep.start()
     advance(ring)
-    advance(ring_out, 2)
     advance(ring)
-    advance(ring_out)
     advance(ring)
     for arrival in arrivals:
         arrival.wait_recv()
@@ -1382,24 +1373,21 @@
     y_copies.finish()
 
 
-def attention_backward(
-    grad_heads, q_all, kv_all, o_all, lse, tops, weights, down_parts, out_left, g_low, given
-):
+def attention_backward(grad_heads, q_all, kv_all, o_all, lse, tops, weights, down_parts, given):
     whole = pl.BlockSpec(memory_space=pltpu.VMEM)
     anywhere = pl.BlockSpec(memory_space=pl.ANY)
     count = 4 + 6 + 6
-    width = g_low.shape[1]
-    down_rows, out_rows = down_parts.shape[3] // 2, out_left.shape[2]
+    width = 2 * given.shape[3]
+    down_rows = down_parts.shape[3] // 2
     return pl.pallas_call(
         backward_kernel,
         out_shape=[
             jax.ShapeDtypeStruct((4, ROWS, 3 * HD), bf16),
             jax.ShapeDtypeStruct((down_rows, width), f32),
-            jax.ShapeDtypeStruct((out_rows, width), f32),
             jax.ShapeDtypeStruct(given.shape, bf16),
         ],
-        in_specs=[whole, whole, anywhere] + [whole] * 3 + [anywhere] * 5,
-        out_specs=[whole] * 3 + [anywhere],
+        in_specs=[whole, whole, anywhere] + [whole] * 3 + [anywhere] * 3,
+        out_specs=[whole] * 2 + [anywhere],
         scratch_shapes=[
             pltpu.VMEM(given.shape, bf16),
             pltpu.VMEM((4, 2, 4, ROWS + CODE_ROWS, 2 * HD), bf16),
@@ -1419,28 +1407,28 @@
             pltpu.SemaphoreType.DMA((3,)),
         ]
         + sum_scratch(2 * given.shape[3])
-        + weight_scratch(down_rows, width)
-        + factor_scratch(out_rows, width)
-        + weight_scratch(out_rows, width),
+        + weight_scratch(down_rows, width),
         compiler_params=pltpu.CompilerParams(
             collective_id=1, has_side_effects=True, vmem_limit_bytes=VMEM_LIMIT
         ),
         name="attention_backward",
     )(
-        grad_heads, q_all, kv_all, o_all, lse, tops, weights, down_parts, out_left, g_low, given
+        grad_heads, q_all, kv_all, o_all, lse, tops, weights, down_parts, given
     )
 
 
 def last_kernel(
     x_ref, labels_ref, gains_ref, packed_ref, cos_ref, sin_ref, gains_two_ref, left_hbm, attn_hbm, mlp_hbm, g_mid_hbm,
-    weight_hbm,
-    input_hbm, layer_hbm, gains_out_ref, grad_qkv_ref,
+    weight_hbm, out_left_hbm, g_low_hbm,
+    input_hbm, layer_hbm, gains_out_ref, grad_qkv_ref, grad_out_ref,
     input_ref, layer_ref, attn, mlp, g_mid, weight, xhat, inverse, given, gains_part, gains_given, came, all_rows, y_send, y_recv, load_sems,
     qkv_left, qkv_right, *more,
 ):
     gain_scratch = more[: len(GAIN_SCRATCH)]
     gain_send, gain_recv = more[len(GAIN_SCRATCH) : len(GAIN_SCRATCH) + 2]
-    qkv_scratch = more[len(GAIN_SCRATCH) + 2 :]
+    qkv_scratch = more[len(GAIN_SCRATCH) + 2 : len(GAIN_SCRATCH) + 9]
+    out_factors = more[len(GAIN_SCRATCH) + 9 : len(GAIN_SCRATCH) + 11]
+    out_scratch = more[len(GAIN_SCRATCH) + 11 :]
     here = place()
     x, y, z, core = here
     loads = []
@@ -1479,8 +1467,12 @@
             qkv_right[0:ROWS, start : start + HD] = grad
     arrived()
     ring = weight_grad(here, grad_qkv_ref, qkv_scratch, (qkv_left, qkv_right))
+    ring_out = weight_grad(
+        here, grad_out_ref, out_scratch, out_factors, left=out_left_hbm, right=g_low_hbm
+    )
     advance(ring)
     loads[0].wait()
+    advance(ring_out)
     for load in loads[1:]:
         load.start()
     copies = Copies(y_send, y_recv)
@@ -1509,6 +1501,7 @@
     advance(ring, 2)
     advance(over_y[0])
     advance(ring, 2)
+    advance(ring_out, 5)
     gains_part[...] = 0.25 * gains_two_ref[...]
 
     def norm(index):
@@ -1530,8 +1523,10 @@
     steps(norm_steps, norm)
     advance(over_y[1])
     advance(over_y[0])
+    advance(ring)
     steps(norm_steps, lambda index: norm(index + norm_steps))
     advance(over_y[1])
+    advance(ring)
     for owner in range(32):
         gains_given[owner // 8, (owner // 2) % 4, owner % 2] = jnp.zeros((8, HD), f32)
         gains_given[owner // 8, (owner // 2) % 4, owner % 2, :, :64] = gains_part[
@@ -1540,6 +1535,9 @@
     gain_copies = Copies(gain_send, gain_recv)
     over_all = sum_gains(gain_copies, here, gains_given, *gain_scratch, gains_out_ref)
     advance(over_all)
+    advance(over_y[0])
+    advance(over_y[1])
+    advance(ring_out, 2)
     advance(ring)
     for load in loads[2:]:
         load.wait()
@@ -1552,15 +1550,12 @@
     steps(ROWS // NORM_ROWS, finish_layer)
     keep = [pltpu.make_async_copy(layer_ref, layer_hbm, load_sems.at[5])]
     keep[0].start()
-    advance(over_y[0])
-    advance(over_all)
-    advance(ring)
-    advance(over_y[1])
     advance(over_all)
     advance(ring)
     advance(over_all)
-    advance(ring)
     advance(over_y[0])
+    advance(ring_out, 2)
+    advance(over_all)
     advance(over_y[1])
 
     def finish_input(index):
@@ -1579,6 +1574,7 @@
         )
         keep[-1].start()
         advance(ring)
+        advance(ring_out)
     advance(over_all)
     for copy in keep:
         copy.wait()
@@ -1587,7 +1583,7 @@
 
 
 def last(
-    activations, labels, gains, packed, cosine, sine, gains_two, left, attn_sum, mlp_sum, g_mid, weight
+    activations, labels, gains, packed, cosine, sine, gains_two, left, attn_sum, mlp_sum, g_mid, weight, out_left, g_low
 ):
     width = activations.shape[1]
     local = weight.shape[2]
@@ -1602,9 +1598,10 @@
             jax.ShapeDtypeStruct((ROWS, width), bf16),
             jax.ShapeDtypeStruct((8, HD), f32),
             jax.ShapeDtypeStruct((3, rows, local), f32),
+            jax.ShapeDtypeStruct((out_left.shape[2], width), f32),
         ],
-        in_specs=[whole] * 7 + [anywhere] * 5,
-        out_specs=[anywhere] * 2 + [whole] * 2,
+        in_specs=[whole] * 7 + [anywhere] * 7,
+        out_specs=[anywhere] * 2 + [whole] * 3,
         scratch_shapes=[
             pltpu.VMEM((ROWS, width), f32),
             pltpu.VMEM((ROWS, width), bf16),
@@ -1623,7 +1620,9 @@
         + factor_scratch(rows, cols)
         + [pltpu.VMEM(shape, f32) for shape in GAIN_SCRATCH]
         + [pltpu.SemaphoreType.DMA((10,)), pltpu.SemaphoreType.DMA((10,))]
-        + weight_scratch(rows, cols),
+        + weight_scratch(rows, cols)
+        + factor_scratch(out_left.shape[2], width)
+        + weight_scratch(out_left.shape[2], width),
         compiler_params=pltpu.CompilerParams(
             collective_id=3, has_side_effects=True, vmem_limit_bytes=VMEM_LIMIT
         ),
@@ -1641,6 +1640,8 @@
         mlp_sum,
         g_mid,
         weight,
+        out_left,
+        g_low,
     )
 
 
@@ -1737,7 +1738,7 @@
         up_weight,
         down_weight,
     )
-    packed, grad_down, grad_out, mlp_sum = attention_backward(
+    packed, grad_down, mlp_sum = attention_backward(
         grad_heads,
         q_all,
         kv_all,
@@ -1746,11 +1747,9 @@
         tops,
         weights,
         down_parts,
-        out_left,
-        g_low,
         mlp_part,
     )
-    grad_input, layer_out, share, grad_qkv = last(
+    grad_input, layer_out, share, grad_qkv, grad_out = last(
         activations,
         label_rows,
         norm_gains,
@@ -1763,6 +1762,8 @@
         mlp_sum,
         g_mid,
         projections,
+        out_left,
+        g_low,
     )
     grad_gains, layer_out, grad_input, grad_qkv, grad_out, grad_up, grad_down = finish(
         norm_gains.shape[0] // 2,

time: 206 us -> 206 us (level)
    pallas_call x1, Pallas kernels: 36.3 us -> 43 us  [last(): pl.pallas_call(last_kernel, out_shape=[jax.ShapeDtypeStruct((ROWS, width)...]
    pallas_call x1, Pallas kernels: 50.8 us -> 45.1 us  [attention_backward(): pl.pallas_call(backward_kernel, out_shape=[jax.ShapeDtypeStruct((4, ROWS,...]
where the time goes in v3:
time: 206 us; the launch traced here: 202 us
  Pallas kernels  202 us (98%)
    pallas_call x1, Pallas kernels, attention_forward(): pl.pallas_call(forward_kernel, out_shape=[jax.ShapeDtypeStruct((2, 4, ROW...  61.8 us
    pallas_call x1, Pallas kernels, middle(): pl.pallas_call(middle_kernel, out_shape=[jax.ShapeDtypeStruct((ROWS, widt...  46.1 us
    pallas_call x1, Pallas kernels, attention_backward(): pl.pallas_call(backward_kernel, out_shape=[jax.ShapeDtypeStruct((4, ROWS,...  45.1 us
    pallas_call x1, Pallas kernels, last(): pl.pallas_call(last_kernel, out_shape=[jax.ShapeDtypeStruct((ROWS, width)...  43 us
    pallas_call x1, Pallas kernels, finish(): pl.pallas_call(finish_kernel, out_shape=[jax.ShapeDtypeStruct((2 * modes,...  5.53 us

profile of v3, /device:TPU:0, one launch (start us, length us, event | category | flops | bytes accessed | tf_op | source)
XLA Modules:
  0.0 202.5 jit_solution(14310154753004636765)
XLA Ops:
  0.6 61.8 %attention_forward.1 = (bf16[2,4,128,128]{3,2,1,0:T(8,128)(2,1)}, bf16[4,2,4,272,256]{4,3,2,1,0:T(8,128)(2,1)}, f32[1024,128]{1,0:T(8,128)}, f32[8,1024]{1,0:T(8...) custom-call(bf16[256,2048]{1,0:T(8,128)(2,1)} %x_ref.5, ...), custom_call_target="tpu_custom_call" | custom-call | tf_op jit(solution)/shard_map/attention_forward/pallas_call | solution.py:850
  62.5 46.1 %middle.1 = (f32[256,2048]{1,0:T(8,128)}, bf16[256,2048]{1,0:T(8,128)(2,1)}, bf16[2,4,128,128]{3,2,1,0:T(8,128)(2,1)}, bf16[2,4,64,1024]{3,2,1,0:T(8,128)(2,1)},...) custom-call(bf16[256,2048]{1,0:T(8,128)(2,1)} %x_ref.5, ...), custom_call_target="tpu_custom_call" | custom-call | tf_op jit(solution)/shard_map/middle/pallas_call | solution.py:1124
  108.6 45.1 %attention_backward.1 = (bf16[4,256,384]{2,1,0:T(8,128)(2,1)}, f32[64,2048]{1,0:T(8,128)}, bf16[2,4,64,1024]{3,2,1,0:T(8,128)(2,1)}) custom-call(bf16[2,4,128,128]{3,2,1,0:T(8,128)(2,1)} %get-tuple-element.47.grads, bf16[2,4,128,128]{3,2,1,0:T(8,128)(2,1)} %get-tuple-element.48.q_ref, bf16[4,2,4,272,256]{4,3,2,1,0:T(8,128)(2,1)} %get-tuple-element.49.kv_hbm, ...), custom_call_target="tpu_custom_call" | custom-call | tf_op jit(solution)/shard_map/attention_backward/pallas_call | solution.py:1382
  153.7 43.0 %last.1 = (f32[256,2048]{1,0:T(8,128)}, bf16[256,2048]{1,0:T(8,128)(2,1)}, f32[8,128]{1,0:T(8,128)}, f32[3,64,512]{2,1,0:T(8,128)}, f32[16,2048]{1,0:T(8,128)}) custom-call(bf16[256,2048]{1,0:T(8,128)(2,1)} %x_ref.5, s32[256,128]{1,0:T(8,128)} %get-tuple-element.43.labels_ref, f32[6,2048]{1,0:T(8,128)} %gains_ref.5, ...), custom_call_target="tpu_custom_call" | custom-call | tf_op jit(solution)/shard_map/last/pallas_call | solution.py:1594
  196.7 5.5 %finish.1 = (f32[6,64]{1,0:T(8,128)}, bf16[256,2048]{1,0:T(8,128)(2,1)}, f32[256,2048]{1,0:T(8,128)}, f32[3,64,512]{2,1,0:T(8,128)}, f32[16,2048]{1,0:T(8,128)}, /*index=5*/f32[64,2048]{1,0:T(8,128)}, f32[64,2048]{1,0:T(8,128)}) custom-call(f32[8,128]{1,0:T(8,128)} %get-tuple-element.65.share_ref, bf16[256,2048]{1,0:T(8,128)(2,1)} %get-tuple-element.66.layer_in, ...), custom_call_target="tpu_custom_call" | custom-call | tf_op jit(solution)/shard_map/finish/pallas_call | solution.py:1681
